TPU v7x, 32 devices: a whole 2x2x4 slice. The times are simulated.
32 devices in a mesh: dp: 8 (over y, x, core), mp: 4 (over z).
Axes of the slice: x: 2, y: 2, z: 4, core: 2. Of those that a mesh axis runs over, the one named last changes fastest.
Arguments:
- inputs: bfloat16 [16384, 1024], P(('dp', 'mp')), may hold values from -6 to 6
- w_query: bfloat16 [1024, 1024], P(None, 'mp'), may hold values from -0.1875 to 0.1875
- w_key: bfloat16 [1024, 1024], P(None, 'mp'), may hold values from -0.1875 to 0.1875
- w_value: bfloat16 [1024, 1024], P(None, 'mp'), may hold values from -0.1875 to 0.1875
- w_gate: bfloat16 [1024, 1024], P(None, 'mp'), may hold values from -0.1875 to 0.1875
- head_gain: float32 [1024], P('mp'), may hold values from 0.1 to 1.9
- w_out: bfloat16 [1024, 1024], P('mp'), may hold values from -0.25 to 0.25
- w_first: bfloat16 [1024, 2816], P(None, 'mp'), may hold values from -0.1875 to 0.1875
- w_second: bfloat16 [1024, 2816], P(None, 'mp'), may hold values from -0.1875 to 0.1875
- w_third: bfloat16 [2816, 1024], P('mp'), may hold values from -0.109375 to 0.109375
- cotangent: bfloat16 [16384, 1024], P(('dp', 'mp')), may hold values from -6 to 6
Outputs:
- output: float32 [16384, 1024], P(('dp', 'mp'))
- grad_inputs: float32 [16384, 1024], P(('dp', 'mp'))
- grad_w_query: float32 [1024, 1024], P(None, 'mp')
- grad_w_key: float32 [1024, 1024], P(None, 'mp')
- grad_w_value: float32 [1024, 1024], P(None, 'mp')
- grad_w_gate: float32 [1024, 1024], P(None, 'mp')
- grad_head_gain: float32 [1024], P('mp')
- grad_w_out: float32 [1024, 1024], P('mp')
- grad_w_first: float32 [1024, 2816], P(None, 'mp')
- grad_w_second: float32 [1024, 2816], P(None, 'mp')
- grad_w_third: float32 [2816, 1024], P('mp')
All inputs are finite; a program needn't handle non-finite values.
Results may differ from a plain program's by a relative error of at most 0.014.
Values may be sent and summed in bfloat16 or wider, within the bound.
A program may use at most 192 MiB of HBM per device.

v0:
```python
import jax
import jax.numpy as jnp
from jax import lax
from jax.sharding import PartitionSpec as P

DH = 64
BLK = 64


EPSILON = 1e-06


def simple_norm(values):
    return values * lax.rsqrt(jnp.mean(values * values, axis=-1, keepdims=True) + EPSILON)


def norm_back(values, gradient):
    factor = lax.rsqrt(jnp.mean(values * values, axis=-1, keepdims=True) + EPSILON)
    normed = values * factor
    return factor * (gradient - normed * jnp.mean(gradient * normed, axis=-1, keepdims=True))


def matmul(left, right):
    return jnp.dot(left, right, preferred_element_type=jnp.float32)


def matmul_tn(left, right):
    return lax.dot_general(
        left, right, (((0,), (0,)), ((), ())), preferred_element_type=jnp.float32
    )


def matmul_nt(left, right):
    return lax.dot_general(
        left, right, (((1,), (1,)), ((), ())), preferred_element_type=jnp.float32
    )


def blocked(matrix):
    return matrix.reshape(matrix.shape[0] // BLK, BLK, matrix.shape[1] // DH, DH)


def attention_weights(queries, key_rows):
    scores = jnp.einsum(
        "bqhd,bkhd->bhqk", blocked(queries), blocked(key_rows), preferred_element_type=jnp.float32
    ) * DH ** (-0.5)
    causal = lax.broadcasted_iota(jnp.int32, (BLK, BLK), 0) >= lax.broadcasted_iota(
        jnp.int32, (BLK, BLK), 1
    )
    scores = jnp.where(causal, scores, -jnp.inf)
    shifted = jnp.exp(scores - jnp.max(scores, axis=-1, keepdims=True))
    return shifted / jnp.sum(shifted, axis=-1, keepdims=True)


def shards(
    inputs, w_query, w_key, w_value, w_gate, head_gain, w_out, w_first, w_second, w_third, cotangent
):
    residual = inputs.astype(jnp.float32)
    attn_in = simple_norm(residual).astype(jnp.bfloat16)
    gathered = lax.all_gather(attn_in, "mp", axis=0, tiled=True)
    queries = matmul(gathered, w_query).astype(jnp.bfloat16)
    key_rows = matmul(gathered, w_key).astype(jnp.bfloat16)
    values = matmul(gathered, w_value).astype(jnp.bfloat16)
    gate_pre = matmul(gathered, w_gate)
    flat_shape = gate_pre.shape
    softmax_out = attention_weights(queries, key_rows)
    softmax_low = softmax_out.astype(jnp.bfloat16)
    attended = jnp.einsum(
        "bhqk,bkhd->bqhd", softmax_low, blocked(values), preferred_element_type=jnp.float32
    )
    per_head = attended.reshape(flat_shape[0], flat_shape[1] // DH, DH)
    factor = lax.rsqrt(jnp.mean(per_head * per_head, axis=-1, keepdims=True) + EPSILON)
    normed = per_head * factor
    normed_flat = normed.reshape(flat_shape)
    activated = jax.nn.silu(gate_pre)
    gated = (normed_flat * head_gain * activated).astype(jnp.bfloat16)
    attn_part = lax.psum_scatter(matmul(gated, w_out), "mp", scatter_dimension=0, tiled=True)
    hidden_res = residual + attn_part
    ffn_in = simple_norm(hidden_res).astype(jnp.bfloat16)
    full_first, full_second, full_third = (w_first, w_second, w_third)
    ffn_rows = lax.all_gather(ffn_in, "mp", axis=0, tiled=True)
    grad_rows = lax.all_gather(cotangent, "mp", axis=0, tiled=True)
    proj_first = matmul(ffn_rows, full_first)
    proj_second = matmul(ffn_rows, full_second)
    product = (proj_first * proj_second).astype(jnp.bfloat16)
    ffn_part = lax.psum_scatter(
        matmul(product, w_third).astype(jnp.bfloat16), "mp", scatter_dimension=0, tiled=True
    ).astype(jnp.float32)
    output = hidden_res + ffn_part
    grad_product = matmul_nt(grad_rows, full_third)
    grad_first = (grad_product * proj_second).astype(jnp.bfloat16)
    grad_second = (grad_product * proj_first).astype(jnp.bfloat16)
    summed = matmul_nt(grad_first, w_first)
    grad_ffn_in = lax.psum_scatter(
        summed + matmul_nt(grad_second, w_second), "mp", scatter_dimension=0, tiled=True
    )
    grad_w_first = matmul_tn(ffn_rows, grad_first)
    grad_w_second = matmul_tn(ffn_rows, grad_second)
    grad_w_third = matmul_tn(product, grad_rows)
    grad_hidden = cotangent.astype(jnp.float32) + norm_back(hidden_res, grad_ffn_in)
    hidden_low = grad_hidden.astype(jnp.bfloat16)
    grad_attn_rows = lax.all_gather(hidden_low, "mp", axis=0, tiled=True)
    grad_gated = matmul_nt(grad_attn_rows, w_out)
    grad_w_out = matmul_tn(gated, grad_attn_rows)
    logistic = jax.nn.sigmoid(gate_pre)
    grad_head_gain = jnp.sum(grad_gated * activated * normed_flat, axis=0)
    grad_gate = (
        grad_gated * normed_flat * head_gain * logistic * (1.0 + gate_pre * (1.0 - logistic))
    ).astype(jnp.bfloat16)
    grad_normed = (grad_gated * activated * head_gain).reshape(normed.shape)
    grad_attended = factor * (
        grad_normed - normed * jnp.mean(grad_normed * normed, axis=-1, keepdims=True)
    )
    grad_blocks = blocked(grad_attended.reshape(flat_shape).astype(jnp.bfloat16))
    grad_values = (
        jnp.einsum("bhqk,bqhd->bkhd", softmax_low, grad_blocks, preferred_element_type=jnp.float32)
        .reshape(flat_shape)
        .astype(jnp.bfloat16)
    )
    grad_softmax = jnp.einsum(
        "bqhd,bkhd->bhqk", grad_blocks, blocked(values), preferred_element_type=jnp.float32
    )
    grad_scores = (
        softmax_out * (grad_softmax - jnp.sum(grad_softmax * softmax_out, axis=-1, keepdims=True))
    ).astype(jnp.bfloat16)
    grad_queries = (
        (
            jnp.einsum(
                "bhqk,bkhd->bqhd",
                grad_scores,
                blocked(key_rows),
                preferred_element_type=jnp.float32,
            )
            * DH ** (-0.5)
        )
        .reshape(flat_shape)
        .astype(jnp.bfloat16)
    )
    grad_keys = (
        (
            jnp.einsum(
                "bhqk,bqhd->bkhd", grad_scores, blocked(queries), preferred_element_type=jnp.float32
            )
            * DH ** (-0.5)
        )
        .reshape(flat_shape)
        .astype(jnp.bfloat16)
    )
    summed = matmul_nt(grad_queries, w_query)
    summed = summed + matmul_nt(grad_keys, w_key)
    summed = summed + matmul_nt(grad_values, w_value)
    grad_attn_in = lax.psum_scatter(
        (summed + matmul_nt(grad_gate, w_gate)).astype(jnp.bfloat16),
        "mp",
        scatter_dimension=0,
        tiled=True,
    ).astype(jnp.float32)
    grad_inputs = grad_hidden + norm_back(residual, grad_attn_in)
    grad_w_query = matmul_tn(gathered, grad_queries)
    grad_w_key = matmul_tn(gathered, grad_keys)
    grad_w_value = matmul_tn(gathered, grad_values)
    grad_w_gate = matmul_tn(gathered, grad_gate)
    (
        grad_w_query,
        grad_w_key,
        grad_w_value,
        grad_w_gate,
        grad_head_gain,
        grad_w_out,
        grad_w_first,
        grad_w_second,
        grad_w_third,
    ) = lax.psum(
        (
            grad_w_query,
            grad_w_key,
            grad_w_value,
            grad_w_gate,
            grad_head_gain,
            grad_w_out,
            grad_w_first,
            grad_w_second,
            grad_w_third,
        ),
        "dp",
    )
    return (
        output,
        grad_inputs,
        grad_w_query,
        grad_w_key,
        grad_w_value,
        grad_w_gate,
        grad_head_gain,
        grad_w_out,
        grad_w_first,
        grad_w_second,
        grad_w_third,
    )


def solution(mesh):
    placed = (
        P(("dp", "mp"), None),
        P(None, "mp"),
        P(None, "mp"),
        P(None, "mp"),
        P(None, "mp"),
        P("mp"),
        P("mp", None),
        P(None, "mp"),
        P(None, "mp"),
        P("mp", None),
        P(("dp", "mp"), None),
    )
    return jax.shard_map(
        shards,
        mesh=mesh,
        in_specs=placed,
        out_specs=(
            P(("dp", "mp"), None),
            P(("dp", "mp"), None),
            P(None, "mp"),
            P(None, "mp"),
            P(None, "mp"),
            P(None, "mp"),
            P("mp"),
            P("mp", None),
            P(None, "mp"),
            P(None, "mp"),
            P("mp", None),
        ),
        check_vma=False,
    )
```

profile of v0, /device:TPU:0, one launch (start us, length us, event | category | flops | bytes accessed | tf_op | source)
XLA Modules:
  0.0 1158.6 jit_solution(4448615826886420335)
XLA Ops:
  7.2 1.7 fusion.8
  8.9 2.4 fusion.4
  11.5 83.5 %all-gather.5.cloned.1.call-done = bf16[2048,1024]{1,0:T(8,128)(2,1)} async-done(((bf16[512,1024]{1,0:T(8,128)(2,1)}), bf16[2048,1024]{1,0:T(8,128)(2,1)}) %all-gather.5.cloned.1.call-update) | async-done | bytes 4194320 | tf_op jit(solution)/shard_map/all_gather | solution.py:60
  95.0 3.4 convolution_convert_fusion.1
  98.4 1.8 reshape.110
  100.3 4.2 copy.103
  104.5 3.4 convolution_convert_fusion.2
  107.9 1.8 reshape.109
  109.7 4.2 copy.107
  113.9 3.4 convolution_convert_fusion.3
  117.4 1.8 reshape.108
  119.2 6.0 fusion.29
  125.2 5.9 multiply_reduce_fusion.1
  131.2 6.7 copy.98
  137.9 5.2 reshape.111
  143.2 5.9 multiply_convert_fusion.7
  149.1 4.6 fusion.32
  153.7 143.1 %reduce-scatter.5.cloned.1.call-done = f32[512,1024]{1,0:T(8,128)} async-done(((f32[2048,1024]{1,0:T(8,128)}), f32[512,1024]{1,0:T(8,128)}) %reduce-scatter.5.cloned.1.call-update) | async-done | bytes 2097168 | tf_op jit(solution)/shard_map/reduce_scatter | solution.py:77
  296.8 2.1 multiply_reduce_fusion.5
  301.0 81.0 %all-gather.7.cloned.1.call-done = bf16[2048,1024]{1,0:T(8,128)(2,1)} async-done(((bf16[512,1024]{1,0:T(8,128)(2,1)}), bf16[2048,1024]{1,0:T(8,128)(2,1)}) %all-gather.7.cloned.1.call-update) | async-done | bytes 4194320 | tf_op jit(solution)/shard_map/all_gather | solution.py:81
  382.0 8.5 fusion.34
  390.5 5.1 fusion.33
  395.5 67.2 %all-gather.9.cloned.1.call-done = bf16[2048,1024]{1,0:T(8,128)(2,1)} async-done(((bf16[512,1024]{1,0:T(8,128)(2,1)}), bf16[2048,1024]{1,0:T(8,128)(2,1)}) %all-gather.9.cloned.1.call-update) | async-done | bytes 4194320 | tf_op jit(solution)/shard_map/all_gather | solution.py:82
  462.8 8.7 multiply_convert_fusion
  471.5 3.5 fusion.35
  475.0 6.0 convolution_add_fusion
  481.1 143.1 %reduce-scatter.9.cloned.1.call-done = f32[512,1024]{1,0:T(8,128)} async-done(((f32[2048,1024]{1,0:T(8,128)}), f32[512,1024]{1,0:T(8,128)}) %reduce-scatter.9.cloned.1.call-update) | async-done | bytes 2097168 | tf_op jit(solution)/shard_map/reduce_scatter | solution.py:94
  624.2 2.8 multiply_reduce_fusion.4
  627.7 1.6 fusion.28
  629.4 16.8 %reshape.113 = f32[2048,4,64]{0,2,1:T(8,128)} reshape(f32[32,64,4,64]{1,0,3,2:T(8,128)} %copy.98) | data formatting | bytes 4194304 | tf_op jit(solution)/shard_map/reshape | solution.py:71
  646.1 64.8 %all-gather.11.cloned.1.call-done = bf16[2048,1024]{1,0:T(8,128)(2,1)} async-done(((bf16[512,1024]{1,0:T(8,128)(2,1)}), bf16[2048,1024]{1,0:T(8,128)(2,1)}) %all-gather.11.cloned.1.call-update) | async-done | bytes 4194320 | tf_op jit(solution)/shard_map/all_gather | solution.py:102
  711.0 5.5 multiply_reduce_fusion.3
  716.6 2.8 multiply_convert_fusion.6
  719.3 4.4 reshape.114
  723.8 4.6 convert_bitcast_fusion
  729.1 2.5 multiply_reduce_fusion
  733.2 2.6 fusion.21
  735.8 2.6 fusion.20
  738.4 2.7 copy.113
  741.0 4.2 convert_element_type.112
  745.3 5.3 copy.106
  750.5 4.2 convert_element_type.106
  754.7 5.6 copy.110
  760.4 4.2 convert_element_type.109
  764.6 2.8 fusion.38
  767.5 4.6 fusion.36
  772.1 4.6 fusion.37
  776.6 9.9 add_convert_fusion
  786.6 7.0 convolution_convert_fusion
  793.9 7.9 fusion.44
  801.8 4.7 fusion.46
  806.6 4.7 fusion.45
  811.3 2.2 fusion.43
  814.3 2.3 fusion.42
  816.6 2.3 fusion.40
  818.9 2.3 fusion.39
  821.2 2.5 fusion.41
  823.7 14.2 %psum.67 = f32[256]{0:T(256)} all-reduce(f32[256]{0:T(256)S(1)} %get-tuple-element.21), channel_id=1, replica_groups=mesh['dp'=8,'mp'=4] {'dp'}, use_global_device_ids=true, to_apply=%region_18.19 | all-reduce | flops 256 | bytes 2048 | tf_op jit(solution)/shard_map/psum | solution.py:173
  837.9 24.2 %reduce-scatter.11.cloned.1.call-done = bf16[512,1024]{1,0:T(8,128)(2,1)} async-done(((bf16[2048,1024]{1,0:T(8,128)(2,1)}), bf16[512,1024]{1,0:T(8,128)(2,1)}) %reduce-scatter.11.cloned.1.call-update) | async-done | bytes 1048592 | tf_op jit(solution)/shard_map/reduce_scatter | solution.py:152
  862.1 1.7 fusion.7
  863.8 78.0 %reduce-scatter.7.cloned.1.call-done = bf16[512,1024]{1,0:T(8,128)(2,1)} async-done(((bf16[2048,1024]{1,0:T(8,128)(2,1)}), bf16[512,1024]{1,0:T(8,128)(2,1)}) %reduce-scatter.7.cloned.1.call-update) | async-done | bytes 1048592 | tf_op jit(solution)/shard_map/reduce_scatter | solution.py:86
  941.8 4.8 fusion.6
  946.6 190.9 %all-reduce.3.cloned.1.call-done = (f32[1024,256]{1,0:T(8,128)}, f32[1024,256]{1,0:T(8,128)}, f32[1024,256]{1,0:T(8,128)}, f32[1024,256]{1,0:T(8,128)}, f32[256,...) async-done(((f32[1024,256]{1,0:T(8,128)}, f32[1024,256]{1,0:T(8,128)}, f32[1024,256]{1,0:T(8,128)}, f32[1024,256]{1,0:T(8,128)}, ...) | async-done | bytes 13893648 | tf_op jit(solution)/shard_map/psum | solution.py:173
  1137.5 2.4 copy.147
  (145 shorter events, 18.4 us)
Async XLA Ops:
  7.2 455.6 %copy-start = (bf16[704,1024]{1,0:T(8,128)(2,1)S(1)}, bf16[704,1024]{1,0:T(8,128)(2,1)}, u32[]{:S(2)}) copy-start(bf16[704,1024]{1,0:T(8,128)(2,1)} %param.20) | copy-start | bytes 4325380
  7.2 87.8 %copy-start.43 = (bf16[1024,256]{1,0:T(8,128)(2,1)S(1)}, bf16[1024,256]{1,0:T(8,128)(2,1)}, u32[]{:S(2)}) copy-start(bf16[1024,256]{1,0:T(8,128)(2,1)} %param.13) | copy-start | bytes 1572868
  7.2 87.8 %all-gather.5.cloned.1.call-start = ((), (), s32[]{:S(2)}) async-start(), calls=%async_computation.4 | async-start | bytes 5242880 | tf_op jit(solution)/shard_map/all_gather | solution.py:60
  8.9 2.5 copy-start.47
  11.4 285.5 %reduce-scatter.5.cloned.1.call-start = ((), (), s32[]{:S(2)}) async-start(), calls=%async_computation.5 | async-start | bytes 10485760 | tf_op jit(solution)/shard_map/reduce_scatter | solution.py:77
  100.3 4.2 copy-start.41
  109.7 4.2 copy-start.40
  125.2 5.9 copy-start.45
  131.2 12.0 %copy-start.38 = (f32[2048,4]{0,1:T(4,128)}, f32[2048,4]{0,1:T(4,128)S(1)}, u32[]{:S(2)}) copy-start(f32[2048,4]{0,1:T(4,128)S(1)} %rsqrt.31) | copy-start | bytes 98308
  137.9 5.3 copy-start.29
  137.9 5.3 copy-start.49
  143.2 5.9 copy-start.31
  149.1 4.6 copy-start.19
  153.7 143.2 %copy-start.1 = (bf16[512,1024]{1,0:T(8,128)(2,1)S(1)}, bf16[512,1024]{1,0:T(8,128)(2,1)}, u32[]{:S(2)}) copy-start(bf16[512,1024]{1,0:T(8,128)(2,1)} %param.11) | copy-start | bytes 3145732
  153.7 228.3 %all-gather.7.cloned.1.call-start = ((), (), s32[]{:S(2)}) async-start(), calls=%async_computation.6 | async-start | bytes 5242880 | tf_op jit(solution)/shard_map/all_gather | solution.py:81
  296.8 2.2 copy-start.2
  300.3 162.4 %all-gather.9.cloned.1.call-start = ((), (), s32[]{:S(2)}) async-start(), calls=%async_computation.8 | async-start | bytes 5242880 | tf_op jit(solution)/shard_map/all_gather | solution.py:82
  300.9 323.3 %reduce-scatter.9.cloned.1.call-start = ((), (), s32[]{:S(2)}) async-start(), calls=%async_computation.9 | async-start | bytes 10485760 | tf_op jit(solution)/shard_map/reduce_scatter | solution.py:94
  382.0 8.5 copy-start.50
  382.0 8.5 copy-start.52
  462.8 8.7 copy-start.53
  471.5 3.5 copy-start.8
  471.5 3.6 copy-start.10
  471.5 3.6 copy-start.54
  481.1 146.0 %copy-start.7 = (bf16[512,1024]{1,0:T(8,128)(2,1)S(1)}, bf16[512,1024]{1,0:T(8,128)(2,1)}, u32[]{:S(2)}) copy-start(bf16[512,1024]{1,0:T(8,128)(2,1)} %param.21) | copy-start | bytes 3145732
  481.1 229.9 %all-gather.11.cloned.1.call-start = ((), (), s32[]{:S(2)}) async-start(), calls=%async_computation.10 | async-start | bytes 5242880 | tf_op jit(solution)/shard_map/all_gather | solution.py:102
  624.2 2.9 copy-start.3
  624.2 3.5 copy-start.6
  629.3 232.8 %reduce-scatter.11.cloned.1.call-start = ((), (), s32[]{:S(2)}) async-start(), calls=%async_computation.11 | async-start | bytes 5242880 | tf_op jit(solution)/shard_map/reduce_scatter | solution.py:152
  711.0 5.6 copy-start.4
  711.0 5.6 copy-start.5
  711.0 5.6 copy-start.39
  723.7 4.6 copy-start.23
  723.7 4.7 copy-start.32
  723.7 5.4 copy-start.33
  723.7 5.4 copy-start.46
  731.6 1.6 copy-start.13
  733.2 2.6 copy-start.12
  764.6 2.8 copy-start.15
  764.6 2.8 copy-start.42
  767.4 4.6 copy-start.17
  767.4 4.6 copy-start.44
  772.1 4.6 copy-start.24
  772.1 4.6 copy-start.30
  786.6 155.2 %reduce-scatter.7.cloned.1.call-start = ((), (), s32[]{:S(2)}) async-start(), calls=%async_computation.7 | async-start | bytes 5242880 | tf_op jit(solution)/shard_map/reduce_scatter | solution.py:86
  793.6 343.9 %all-reduce.3.cloned.1.call-start = ((), (), s32[]{:S(2)}) async-start(), calls=%async_computation.12 | async-start | bytes 27787264 | tf_op jit(solution)/shard_map/psum | solution.py:173
  793.9 8.0 copy-start.11
  793.9 8.0 copy-start.51
  801.8 4.8 copy-start.9
  806.6 4.8 copy-start.20
  806.6 4.8 copy-start.22
  811.3 2.3 copy-start.21
  811.3 2.9 copy-start.25
  814.3 2.3 copy-start.18
  816.6 2.3 copy-start.16
  818.9 2.3 copy-start.14
  823.7 38.4 %copy-start.48 = (f32[512]{0:T(512)S(1)}, f32[512]{0:T(512)}, u32[]{:S(2)}) copy-start(f32[512]{0:T(512)} %copy-done.47) | copy-start | bytes 6148
  1137.5 2.4 copy-start.37
  1137.5 3.4 copy-start.36
  1139.9 1.9 copy-start.35
  1140.9 1.9 copy-start.34
  1141.9 2.7 copy-start.28
  1144.5 2.9 copy-start.27
  1147.4 2.9 copy-start.26
Sparse Core Ops, SparseCore 0:
  11.5 83.4 all-gather.4
  153.8 142.9 reduce-scatter.4
  300.5 81.4 all-gather.6
  383.4 79.2 all-gather.8
  481.2 142.9 reduce-scatter.8
  629.4 81.4 all-gather.10
  786.7 75.2 reduce-scatter.10
  864.5 77.2 reduce-scatter.6
  947.7 189.7 all-reduce.2
where the time goes:
time: 1170 us; the launch traced here: 1160 us
  waiting for transfers between devices  876 us (75%)
  matrix products  140 us (12%)
  local copies, waits for them, and re-layouts  90.2 us (8%)
  other arithmetic  22.5 us (2%)
  between operations  14.5 us (1%)
  blocking collectives  14.2 us (1%)
    psum x1, waiting for transfers between devices, shards(): lax.psum((grad_w_query, grad_w_key, grad_w_value, grad_w_gate, grad_head_...  191 us
    reduce_scatter x1, waiting for transfers between devices, shards(): lax.psum_scatter(matmul(gated, w_out), 'mp', scatter_dimension=0, tiled=T...  143 us
    reduce_scatter x1, waiting for transfers between devices, shards(): lax.psum_scatter(summed + matmul_nt(grad_second, w_second), 'mp', scatter...  143 us
    all_gather x1, waiting for transfers between devices, shards(): gathered = lax.all_gather(attn_in, 'mp', axis=0, tiled=True)  83.5 us
    all_gather x1, waiting for transfers between devices, shards(): ffn_rows = lax.all_gather(ffn_in, 'mp', axis=0, tiled=True)  81 us
    reduce_scatter x1, waiting for transfers between devices, shards(): lax.psum_scatter(matmul(product, w_third).astype(jnp.bfloat16), 'mp', sca...  78 us
    all_gather x1, waiting for transfers between devices, shards(): grad_rows = lax.all_gather(cotangent, 'mp', axis=0, tiled=True)  67.2 us
    all_gather x1, waiting for transfers between devices, shards(): grad_attn_rows = lax.all_gather(hidden_low, 'mp', axis=0, tiled=True)  64.8 us
  transfers between devices with their start and end apart: 9, of which 9 were waited for; matrix products, arithmetic and copies ran while one was open for 6% of the time, Pallas kernels for 0%

commit v1 on v0

v1 whole, which is shorter than its diff:
```python
import jax
import jax.numpy as jnp
from jax import lax
from jax.sharding import PartitionSpec as P

DH = 64
BLK = 64


EPSILON = 1e-06


def simple_norm(values):
    return values * lax.rsqrt(jnp.mean(values * values, axis=-1, keepdims=True) + EPSILON)


def norm_back(values, gradient):
    factor = lax.rsqrt(jnp.mean(values * values, axis=-1, keepdims=True) + EPSILON)
    normed = values * factor
    return factor * (gradient - normed * jnp.mean(gradient * normed, axis=-1, keepdims=True))


def matmul(left, right):
    return jnp.dot(left, right, preferred_element_type=jnp.float32)


def matmul_tn(left, right):
    return lax.dot_general(
        left, right, (((0,), (0,)), ((), ())), preferred_element_type=jnp.float32
    )


def matmul_nt(left, right):
    return lax.dot_general(
        left, right, (((1,), (1,)), ((), ())), preferred_element_type=jnp.float32
    )


def blocked(matrix):
    return matrix.reshape(matrix.shape[0] // BLK, BLK, matrix.shape[1] // DH, DH)


def attention_weights(queries, key_rows):
    scores = jnp.einsum(
        "bqhd,bkhd->bhqk", blocked(queries), blocked(key_rows), preferred_element_type=jnp.float32
    ) * DH ** (-0.5)
    causal = lax.broadcasted_iota(jnp.int32, (BLK, BLK), 0) >= lax.broadcasted_iota(
        jnp.int32, (BLK, BLK), 1
    )
    scores = jnp.where(causal, scores, -jnp.inf)
    shifted = jnp.exp(scores - jnp.max(scores, axis=-1, keepdims=True))
    return shifted / jnp.sum(shifted, axis=-1, keepdims=True)


ALL = ("mp", "dp")


def gather_weight(weight):
    rows = weight.shape[0] // lax.axis_size("dp")
    part = lax.dynamic_slice_in_dim(weight, lax.axis_index("dp") * rows, rows, 0)
    full = lax.all_gather(part, ALL, axis=0, tiled=True)
    return full.reshape(lax.axis_size("mp"), weight.shape[0], weight.shape[1])


def reduce_gradient(stacked):
    shards_, rows, columns = stacked.shape
    part = lax.psum_scatter(stacked.reshape(shards_ * rows, columns), ALL, scatter_dimension=0, tiled=True)
    return lax.all_gather(part, "dp", axis=0, tiled=True)


def shards(
    inputs, w_query, w_key, w_value, w_gate, head_gain, w_out, w_first, w_second, w_third, cotangent
):
    low = jnp.bfloat16
    parts = lax.axis_size("mp")
    heads_wide = w_query.shape[1]
    w_in = gather_weight(jnp.concatenate([w_query, w_key, w_value, w_gate], axis=1))
    full_out = gather_weight(w_out).reshape(-1, w_out.shape[1])
    full_first = gather_weight(w_first)
    full_second = gather_weight(w_second)
    full_third = gather_weight(w_third).reshape(-1, w_third.shape[1])
    gain = lax.all_gather(head_gain, "mp", axis=0, tiled=True)

    residual = inputs.astype(jnp.float32)
    attn_in = simple_norm(residual).astype(low)
    proj = [matmul(attn_in, w_in[m]) for m in range(parts)]

    def field(i):
        return jnp.concatenate([p[:, i * heads_wide : (i + 1) * heads_wide] for p in proj], axis=1)

    queries = field(0).astype(low)
    key_rows = field(1).astype(low)
    values = field(2).astype(low)
    gate_pre = field(3)
    flat_shape = gate_pre.shape
    softmax_out = attention_weights(queries, key_rows)
    softmax_low = softmax_out.astype(low)
    attended = jnp.einsum(
        "bhqk,bkhd->bqhd", softmax_low, blocked(values), preferred_element_type=jnp.float32
    )
    per_head = attended.reshape(flat_shape[0], flat_shape[1] // DH, DH)
    factor = lax.rsqrt(jnp.mean(per_head * per_head, axis=-1, keepdims=True) + EPSILON)
    normed = per_head * factor
    normed_flat = normed.reshape(flat_shape)
    activated = jax.nn.silu(gate_pre)
    gated = (normed_flat * gain * activated).astype(low)
    hidden_res = residual + matmul(gated, full_out)
    ffn_in = simple_norm(hidden_res).astype(low)
    proj_first = jnp.concatenate([matmul(ffn_in, full_first[m]) for m in range(parts)], axis=1)
    proj_second = jnp.concatenate([matmul(ffn_in, full_second[m]) for m in range(parts)], axis=1)
    product = (proj_first * proj_second).astype(low)
    output = hidden_res + matmul(product, full_third)
    grad_product = matmul_nt(cotangent, full_third)
    grad_first = (grad_product * proj_second).astype(low)
    grad_second = (grad_product * proj_first).astype(low)
    hidden_part = w_first.shape[1]

    def cut(array, m, width):
        return array[:, m * width : (m + 1) * width]

    grad_ffn_in = sum(
        matmul_nt(cut(grad_first, m, hidden_part), full_first[m])
        + matmul_nt(cut(grad_second, m, hidden_part), full_second[m])
        for m in range(parts)
    )
    grad_w_third = reduce_gradient(matmul_tn(product, cotangent).astype(low).reshape(parts, hidden_part, -1))
    grad_w_first = reduce_gradient(
        jnp.stack([matmul_tn(ffn_in, cut(grad_first, m, hidden_part)).astype(low) for m in range(parts)])
    )
    grad_w_second = reduce_gradient(
        jnp.stack([matmul_tn(ffn_in, cut(grad_second, m, hidden_part)).astype(low) for m in range(parts)])
    )
    grad_hidden = cotangent.astype(jnp.float32) + norm_back(hidden_res, grad_ffn_in)
    hidden_low = grad_hidden.astype(low)
    grad_gated = matmul_nt(hidden_low, full_out)
    grad_w_out = reduce_gradient(matmul_tn(gated, hidden_low).astype(low).reshape(parts, heads_wide, -1))
    logistic = jax.nn.sigmoid(gate_pre)
    grad_head_gain = jnp.sum(grad_gated * activated * normed_flat, axis=0)
    grad_gate = (
        grad_gated * normed_flat * gain * logistic * (1.0 + gate_pre * (1.0 - logistic))
    ).astype(low)
    grad_normed = (grad_gated * activated * gain).reshape(normed.shape)
    grad_attended = factor * (
        grad_normed - normed * jnp.mean(grad_normed * normed, axis=-1, keepdims=True)
    )
    grad_blocks = blocked(grad_attended.reshape(flat_shape).astype(low))
    grad_values = (
        jnp.einsum("bhqk,bqhd->bkhd", softmax_low, grad_blocks, preferred_element_type=jnp.float32)
        .reshape(flat_shape)
        .astype(low)
    )
    grad_softmax = jnp.einsum(
        "bqhd,bkhd->bhqk", grad_blocks, blocked(values), preferred_element_type=jnp.float32
    )
    grad_scores = (
        softmax_out * (grad_softmax - jnp.sum(grad_softmax * softmax_out, axis=-1, keepdims=True))
    ).astype(low)
    grad_queries = (
        (
            jnp.einsum("bhqk,bkhd->bqhd", grad_scores, blocked(key_rows), preferred_element_type=jnp.float32)
            * DH ** (-0.5)
        )
        .reshape(flat_shape)
        .astype(low)
    )
    grad_keys = (
        (
            jnp.einsum("bhqk,bqhd->bkhd", grad_scores, blocked(queries), preferred_element_type=jnp.float32)
            * DH ** (-0.5)
        )
        .reshape(flat_shape)
        .astype(low)
    )
    grad_proj = [
        jnp.concatenate(
            [cut(g, m, heads_wide) for g in (grad_queries, grad_keys, grad_values, grad_gate)], axis=1
        )
        for m in range(parts)
    ]
    grad_attn_in = sum(matmul_nt(grad_proj[m], w_in[m]) for m in range(parts))
    grad_inputs = grad_hidden + norm_back(residual, grad_attn_in)
    grad_w_in = reduce_gradient(jnp.stack([matmul_tn(attn_in, grad_proj[m]).astype(low) for m in range(parts)]))
    grad_head_gain = lax.psum(grad_head_gain, ALL)
    grad_head_gain = lax.dynamic_slice_in_dim(grad_head_gain, lax.axis_index("mp") * heads_wide, heads_wide, 0)
    wide = jnp.float32
    return (
        output,
        grad_inputs,
        cut(grad_w_in, 0, heads_wide).astype(wide),
        cut(grad_w_in, 1, heads_wide).astype(wide),
        cut(grad_w_in, 2, heads_wide).astype(wide),
        cut(grad_w_in, 3, heads_wide).astype(wide),
        grad_head_gain,
        grad_w_out.astype(wide),
        grad_w_first.astype(wide),
        grad_w_second.astype(wide),
        grad_w_third.astype(wide),
    )


def solution(mesh):
    placed = (
        P(("dp", "mp"), None),
        P(None, "mp"),
        P(None, "mp"),
        P(None, "mp"),
        P(None, "mp"),
        P("mp"),
        P("mp", None),
        P(None, "mp"),
        P(None, "mp"),
        P("mp", None),
        P(("dp", "mp"), None),
    )
    return jax.shard_map(
        shards,
        mesh=mesh,
        in_specs=placed,
        out_specs=(
            P(("dp", "mp"), None),
            P(("dp", "mp"), None),
            P(None, "mp"),
            P(None, "mp"),
            P(None, "mp"),
            P(None, "mp"),
            P("mp"),
            P("mp", None),
            P(None, "mp"),
            P(None, "mp"),
            P("mp", None),
        ),
        check_vma=False,
    )
```

time: 1170 us -> 1190 us (1.017)
  waiting for transfers between devices: 876 us -> 806 us
  blocking collectives: 14.2 us -> 60 us
  local copies, waits for them, and re-layouts: 90.2 us -> 122 us
  other arithmetic: 22.5 us -> 47.7 us
  matrix products: 140 us -> 127 us
    psum x1 -> x0, waiting for transfers between devices: 191 us -> none  [shards(): lax.psum((grad_w_query, grad_w_key, grad_w_value, grad_w_gate, grad_head_...]
    unnamed x9 -> x16, waiting for transfers between devices: 0.65 us -> 95.9 us
    all_gather x4 -> x9, waiting for transfers between devices: 297 us -> 339 us  [the longest x5 253 us: gather_weight(): full = lax.all_gather(part, ALL, axis=0, tiled=True)]
    psum x1, blocking collectives: 14.2 us -> 37.3 us  [shards(): grad_head_gain = lax.psum(grad_head_gain, ALL)]
    all_gather x0 -> x2, blocking collectives: none -> 22.7 us  [the longest x1 12.7 us: shards(): gain = lax.all_gather(head_gain, 'mp', axis=0, tiled=True)]
    convert_element_type x0 -> x5, local copies, waits for them, and re-layouts: none -> 18.6 us  [the longest x2 8.47 us: shards(): key_rows = field(1).astype(low)]
    reduce_scatter x4 -> x3, waiting for transfers between devices: 388 us -> 371 us  [reduce_gradient(): lax.psum_scatter(stacked.reshape(shards_ * rows, columns), ALL, scatter_d...]
    convert_element_type x4 -> x8, other arithmetic: 8.03 us -> 24.9 us  [the longest x1 5.57 us: shards(): gated = (normed_flat * gain * activated).astype(low)]
  transfers between devices with their start and end apart: 9 -> 14, of which waited for: 9 -> 12; matrix products, arithmetic and copies ran while one was open for 6% -> 22% of each run, Pallas kernels for 0% -> 0%
where the time goes in v1:
time: 1190 us; the launch traced here: 1180 us
  waiting for transfers between devices  806 us (68%)
  matrix products  127 us (11%)
  local copies, waits for them, and re-layouts  122 us (10%)
  blocking collectives  60 us (5%)
  other arithmetic  47.7 us (4%)
  between operations  15.2 us (1%)
    reduce_scatter x3, waiting for transfers between devices, reduce_gradient(): lax.psum_scatter(stacked.reshape(shards_ * rows, columns), ALL, scatter_d...  371 us
    all_gather x5, waiting for transfers between devices, gather_weight(): full = lax.all_gather(part, ALL, axis=0, tiled=True)  253 us
    unnamed x16, waiting for transfers between devices  95.9 us
    all_gather x4, waiting for transfers between devices, reduce_gradient(): return lax.all_gather(part, 'dp', axis=0, tiled=True)  86.4 us
    dot_general x14, matrix products, matmul_nt(): lax.dot_general(left, right, (((1,), (1,)), ((), ())), preferred_element_...  37.6 us
    psum x1, blocking collectives, shards(): grad_head_gain = lax.psum(grad_head_gain, ALL)  37.3 us
    dot_general x14, matrix products, matmul(): return jnp.dot(left, right, preferred_element_type=jnp.float32)  35.7 us
    dot_general x14, matrix products, matmul_tn(): lax.dot_general(left, right, (((0,), (0,)), ((), ())), preferred_element_...  27.3 us
  transfers between devices with their start and end apart: 14, of which 12 were waited for; matrix products, arithmetic and copies ran while one was open for 22% of the time, Pallas kernels for 0%

profile of v1, /device:TPU:0, one launch (start us, length us, event | category | flops | bytes accessed | tf_op | source)
XLA Modules:
  0.0 1179.2 jit_solution(116495958480606439)
XLA Ops:
  14.9 12.7 %all-gather = f32[4,1,256]{2,1,0:T(1,128)S(1)} all-gather(f32[1,1,256]{2,1,0:T(1,128)S(1)} %bitcast.111), channel_id=1, replica_groups=mesh['dp'=8,'mp'=4] {'mp'}, dimensions={0}, use_global_device_ids=true | all-gather | bytes 5120 | tf_op jit(solution)/shard_map/all_gather | solution.py:82
  27.9 63.7 %all-gather.11.cloned.1.call-done = bf16[4096,1024]{1,0:T(8,128)(2,1)} async-done(((bf16[128,1024]{1,0:T(8,128)(2,1)}), bf16[4096,1024]{1,0:T(8,128)(2,1)}) %all-gather.11.cloned.1.call-update) | async-done | bytes 8388624 | tf_op jit(solution)/shard_map/all_gather | solution.py:61
  91.6 3.0 fusion.128
  108.1 3.7 copy.107
  111.8 2.8 pad_maximum_fusion.8
  114.6 4.0 convert_element_type.151
  118.6 4.5 copy.103
  123.1 4.0 convert_element_type.149
  127.1 5.4 fusion.132
  132.4 6.2 multiply_reduce_fusion.1
  138.6 5.6 copy.94
  144.2 4.9 reshape.144
  152.9 5.6 multiply_convert_fusion.6
  158.5 3.4 multiply_reduce_fusion.5
  162.1 65.5 %all-gather.15.cloned.1.call-done = bf16[4096,704]{0,1:T(8,128)(2,1)} async-done(((bf16[128,704]{0,1:T(8,128)(2,1)}), bf16[4096,704]{0,1:T(8,128)(2,1)}) %all-gather.15.cloned.1.call-update) | async-done | bytes 5767184 | tf_op jit(solution)/shard_map/all_gather | solution.py:61
  227.6 3.6 fusion.62
  237.3 66.9 %all-gather.17.cloned.1.call-done = bf16[4096,704]{0,1:T(8,128)(2,1)} async-done(((bf16[128,704]{0,1:T(8,128)(2,1)}), bf16[4096,704]{0,1:T(8,128)(2,1)}) %all-gather.17.cloned.1.call-update) | async-done | bytes 5767184 | tf_op jit(solution)/shard_map/all_gather | solution.py:61
  304.3 3.6 fusion.46
  312.0 3.4 fusion.58
  315.4 57.0 %all-gather.19.cloned.1.call-done = bf16[2816,1024]{1,0:T(8,128)(2,1)} async-done(((bf16[88,1024]{1,0:T(8,128)(2,1)}), bf16[2816,1024]{1,0:T(8,128)(2,1)}) %all-gather.19.cloned.1.call-update) | async-done | bytes 5767184 | tf_op jit(solution)/shard_map/all_gather | solution.py:61
  372.4 10.5 fusion.2
  388.0 3.1 pad_maximum_fusion.3
  391.1 8.4 copy.126
  405.0 3.1 pad_maximum_fusion.4
  408.1 8.6 copy.127
  416.7 7.6 copy.98
  424.3 5.1 reshape.146
  429.3 6.9 convolution_convert_fusion
  436.3 2.8 fusion.60
  441.7 2.9 fusion.48
  454.2 3.8 multiply_reduce_fusion.2
  457.9 2.9 copy.97
  460.8 2.8 multiply_reduce_fusion.3
  465.4 2.9 copy.99
  468.3 4.4 multiply_convert_fusion.5
  475.0 4.4 copy.111
  479.4 5.4 convert_bitcast_fusion.4
  484.8 4.4 copy.113
  489.2 3.5 convert_element_type.170
  492.7 4.9 multiply_reduce_fusion
  500.5 2.7 copy.110
  503.2 4.1 convert_element_type.167
  507.3 3.5 fusion.35
  510.9 2.8 copy.106
  513.6 4.5 convert_element_type.164
  527.5 3.9 pad_maximum_fusion
  531.5 4.6 convolution_convert_fusion.1
  538.1 95.7 %reduce-scatter.18.cloned.1.call-done = bf16[128,704]{1,0:T(8,128)(2,1)} async-done(((bf16[4096,704]{1,0:T(8,128)(2,1)}), bf16[128,704]{1,0:T(8,128)(2,1)}) %reduce-scatter.18.cloned.1.call-update) | async-done | bytes 180240
  635.5 143.5 %reduce-scatter.14.cloned.1.call-done = bf16[88,1024]{1,0:T(8,128)(2,1)} async-done(((bf16[2816,1024]{1,0:T(8,128)(2,1)}), bf16[88,1024]{1,0:T(8,128)(2,1)}) %reduce-scatter.14.cloned.1.call-update) | async-done | bytes 180240 | tf_op jit(solution)/shard_map/reduce_scatter | solution.py:67
  779.1 146.8 %reduce-scatter.10.cloned.1.call-done = bf16[128,1024]{1,0:T(8,128)(2,1)} async-done(((bf16[4096,1024]{1,0:T(8,128)(2,1)}), bf16[128,1024]{1,0:T(8,128)(2,1)}) %reduce-scatter.10.cloned.1.call-update) | async-done | bytes 262160 | tf_op jit(solution)/shard_map/reduce_scatter | solution.py:67
  926.0 37.3 %psum.7 = f32[1024]{0:T(1024)S(1)} all-reduce(f32[1024]{0:T(1024)S(1)} %get-tuple-element.13), channel_id=1, replica_groups=mesh['dp'=8,'mp'=4] {'mp','dp'}, use_global_device_ids=true, to_apply=%region_11.12 | all-reduce | flops 1024 | bytes 8192 | tf_op jit(solution)/shard_map/psum | solution.py:183
  963.9 3.4 fusion.16
  967.4 3.0 fusion.20
  976.3 4.5 convolution_add_fusion
  980.8 80.6 %reduce-scatter.12.cloned.1.call-done = bf16[32,1024]{1,0:T(8,128)(2,1)} async-done(((bf16[1024,1024]{1,0:T(8,128)(2,1)}), bf16[32,1024]{1,0:T(8,128)(2,1)}) %reduce-scatter.12.cloned.1.call-update) | async-done | bytes 65552 | tf_op jit(solution)/shard_map/reduce_scatter | solution.py:67
  1061.4 10.0 all_gather.40
  1072.4 12.2 %all-gather.23.cloned.1.call-done = bf16[1024,704]{0,1:T(8,128)(2,1)} async-done(((bf16[128,704]{0,1:T(8,128)(2,1)}), bf16[1024,704]{0,1:T(8,128)(2,1)}) %all-gather.23.cloned.1.call-update) | async-done | bytes 1441808 | tf_op jit(solution)/shard_map/all_gather | solution.py:68
  1084.6 3.3 convert_element_type.186
  1087.9 23.9 %all-gather.25.cloned.1.call-done = bf16[1024,704]{0,1:T(8,128)(2,1)} async-done(((bf16[128,704]{0,1:T(8,128)(2,1)}), bf16[1024,704]{0,1:T(8,128)(2,1)}) %all-gather.25.cloned.1.call-update) | async-done | bytes 1441808 | tf_op jit(solution)/shard_map/all_gather | solution.py:68
  1111.8 3.3 convert_element_type.191
  1115.1 23.9 %all-gather.27.cloned.1.call-done = bf16[704,1024]{1,0:T(8,128)(2,1)} async-done(((bf16[88,1024]{1,0:T(8,128)(2,1)}), bf16[704,1024]{1,0:T(8,128)(2,1)}) %all-gather.27.cloned.1.call-update) | async-done | bytes 1441808 | tf_op jit(solution)/shard_map/all_gather | solution.py:68
  1139.1 3.4 convert_element_type.193
  1142.5 26.4 %all-gather.21.cloned.1.call-done = bf16[1024,1024]{1,0:T(8,128)(2,1)} async-done(((bf16[128,1024]{1,0:T(8,128)(2,1)}), bf16[1024,1024]{1,0:T(8,128)(2,1)}) %all-gather.21.cloned.1.call-update) | async-done | bytes 2097168 | tf_op jit(solution)/shard_map/all_gather | solution.py:68
  1168.9 3.6 slice_convert_fusion
  (240 shorter events, 85.5 us)
Async XLA Ops:
  7.2 3.5 copy-start
  7.2 84.4 %all-gather.11.cloned.1.call-start = ((), (), s32[]{:S(2)}) async-start(), calls=%async_computation.5 | async-start | bytes 8650752 | tf_op jit(solution)/shard_map/all_gather | solution.py:61
  7.2 7.7 copy-start.54
  7.3 20.4 %copy-start.10 = (bf16[512,1024]{1,0:T(8,128)(2,1)S(1)}, bf16[512,1024]{1,0:T(8,128)(2,1)}, u32[]{:S(2)}) copy-start(bf16[512,1024]{1,0:T(8,128)(2,1)} %param.11) | copy-start | bytes 3145732
  9.1 149.4 %all-gather.13.cloned.1.call-start = ((), (), s32[]{:S(2)}) async-start(), calls=%async_computation.6 | async-start | bytes 2162688 | tf_op jit(solution)/shard_map/all_gather | solution.py:61
  10.7 216.9 %all-gather.15.cloned.1.call-start = ((), (), s32[]{:S(2)}) async-start(), calls=%async_computation.7 | async-start | bytes 5947392 | tf_op jit(solution)/shard_map/all_gather | solution.py:61
  11.5 292.8 %all-gather.17.cloned.1.call-start = ((), (), s32[]{:S(2)}) async-start(), calls=%async_computation.8 | async-start | bytes 5947392 | tf_op jit(solution)/shard_map/all_gather | solution.py:61
  13.2 359.3 %all-gather.19.cloned.1.call-start = ((), (), s32[]{:S(2)}) async-start(), calls=%async_computation.9 | async-start | bytes 5947392 | tf_op jit(solution)/shard_map/all_gather | solution.py:61
  14.8 521.4 %reduce-scatter.16.cloned.1.call-start = ((), (), s32[]{:S(2)}) async-start(), calls=%async_computation.17 | async-start | bytes 6488064
  27.9 72.0 %copy-start.52 = (f32[512]{0:T(512)}, f32[512]{0:T(512)S(1)}, u32[]{:S(2)}) copy-start(f32[512]{0:T(512)S(1)} %add_rsqrt_fusion.2) | copy-start | bytes 6148
  91.6 4.0 copy-start.55
  111.8 15.3 %copy-start.6 = (bf16[8,64,16,64]{1,3,2,0:T(8,128)(2,1)}, bf16[8,64,16,64]{1,3,2,0:T(8,128)(2,1)S(1)}, u32[]{:S(2)}) copy-start(bf16[8,64,16,64]{1,3,2,0:T(8,128)(2,1)S(1)} %copy.107) | copy-start | bytes 3145732
  152.9 5.6 copy-start.3
  162.1 147.9 %copy-start.20 = (bf16[512,1024]{1,0:T(8,128)(2,1)}, bf16[512,1024]{1,0:T(8,128)(2,1)S(1)}, u32[]{:S(2)}) copy-start(bf16[512,1024]{1,0:T(8,128)(2,1)S(1)} %multiply_convert_fusion.7) | copy-start | bytes 3145732
  227.6 3.6 copy-start.56
  304.3 3.6 copy-start.23
  312.0 60.4 %copy-start.19 = (bf16[512,1024]{1,0:T(8,128)(2,1)S(1)}, bf16[512,1024]{1,0:T(8,128)(2,1)}, u32[]{:S(2)}) copy-start(bf16[512,1024]{1,0:T(8,128)(2,1)} %param.21) | copy-start | bytes 3145732
  372.4 10.6 copy-start.21
  383.0 2.2 copy-start.58
  399.5 234.2 %reduce-scatter.18.cloned.1.call-start = ((), (), s32[]{:S(2)}) async-start(), calls=%async_computation.18 | async-start | bytes 6488064
  399.6 2.5 copy-start.22
  399.6 2.7 copy-start.50
  416.7 362.4 %reduce-scatter.14.cloned.1.call-start = ((), (), s32[]{:S(2)}) async-start(), calls=%async_computation.15 | async-start | bytes 5947392 | tf_op jit(solution)/shard_map/reduce_scatter | solution.py:67
  436.3 489.7 %reduce-scatter.10.cloned.1.call-start = ((), (), s32[]{:S(2)}) async-start(), calls=%async_computation.10 | async-start | bytes 8650752 | tf_op jit(solution)/shard_map/reduce_scatter | solution.py:67
  436.3 2.8 copy-start.59
  436.3 8.3 slice-start.6
  439.2 2.6 copy-start.51
  439.2 5.4 slice-start.7
  439.2 6.5 slice-start.2
  441.7 3.9 slice-start.3
  450.6 2.6 copy-start.16
  450.6 2.7 copy-start.17
  450.6 2.9 copy-start.18
  450.6 3.6 copy-start.57
  451.1 6.8 copy-start.4
  492.7 4.9 copy-start.14
  519.5 3.6 copy-start.30
  519.6 5.1 copy-start.26
  519.7 3.5 copy-start.37
  519.7 4.9 copy-start.32
  519.7 6.3 copy-start.24
  521.5 3.2 copy-start.39
  521.5 4.6 copy-start.28
  521.6 3.1 copy-start.44
  521.6 4.5 copy-start.35
  531.4 529.9 %reduce-scatter.12.cloned.1.call-start = ((), (), s32[]{:S(2)}) async-start(), calls=%async_computation.12 | async-start | bytes 2162688 | tf_op jit(solution)/shard_map/reduce_scatter | solution.py:67
  536.1 548.5 %all-gather.23.cloned.1.call-start = ((), (), s32[]{:S(2)}) async-start(), calls=%async_computation.13 | async-start | bytes 1622016 | tf_op jit(solution)/shard_map/all_gather | solution.py:68
  538.0 573.8 %all-gather.25.cloned.1.call-start = ((), (), s32[]{:S(2)}) async-start(), calls=%async_computation.14 | async-start | bytes 1622016 | tf_op jit(solution)/shard_map/all_gather | solution.py:68
  635.5 503.6 %all-gather.27.cloned.1.call-start = ((), (), s32[]{:S(2)}) async-start(), calls=%async_computation.16 | async-start | bytes 1622016 | tf_op jit(solution)/shard_map/all_gather | solution.py:68
  779.1 389.8 %all-gather.21.cloned.1.call-start = ((), (), s32[]{:S(2)}) async-start(), calls=%async_computation.11 | async-start | bytes 2359296 | tf_op jit(solution)/shard_map/all_gather | solution.py:68
  963.9 3.4 copy-start.31
  963.9 3.4 copy-start.38
  963.9 3.4 copy-start.43
  963.9 3.4 copy-start.48
  963.9 6.5 slice-start.4
  967.3 3.1 copy-start.27
  967.3 3.1 copy-start.33
  967.3 3.1 copy-start.40
  967.4 3.1 copy-start.45
  967.4 3.1 slice-start.5
  970.5 4.9 slice-start
  971.9 3.5 slice-start.1
  973.6 2.7 copy-start.9
  1139.1 33.5 %copy-start.1 = (bf16[1024,704]{0,1:T(8,128)(2,1)S(1)}, bf16[1024,704]{0,1:T(8,128)(2,1)}, u32[]{:S(2)}) copy-start(bf16[1024,704]{0,1:T(8,128)(2,1)} %param.18) | copy-start | bytes 4325380
  (18 other events, 30.5 us)
Sparse Core Ops, SparseCore 0:
  11.5 80.0 all-gather.10
  94.5 54.9 all-gather.12
  152.9 74.6 all-gather.14
  230.3 73.9 all-gather.16
  306.9 65.4 all-gather.18
  399.7 113.5 reduce-scatter.15
  519.8 113.8 reduce-scatter.17
  636.0 142.9 reduce-scatter.13
  781.3 144.5 reduce-scatter.9
  928.6 132.7 reduce-scatter.11
  1063.4 21.1 all-gather.22
  1086.5 25.2 all-gather.24
  1113.9 25.1 all-gather.26
  1141.0 27.8 all-gather.20

commit v2 on v1

--- a/solution.py
+++ b/solution.py
@@ -1,6 +1,10 @@
+import functools
+
 import jax
 import jax.numpy as jnp
 from jax import lax
+from jax.experimental import pallas as pl
+from jax.experimental.pallas import tpu as pltpu
 from jax.sharding import PartitionSpec as P
 
 DH = 64
@@ -55,6 +59,121 @@
 ALL = ("mp", "dp")
 
 
+MESH = pl.DeviceIdType.MESH
+W = [(1024,256)]*4 + [(256,1024), (1024,704),(1024,704),(704,1024)]
+CH = [(0,0,0,0,256),(1,0,256,0,256),(2,0,512,0,256),(3,0,768,0,256),(4,1,0,0,64),(5,2,0,0,128),(5,2,0,128,128),(6,3,0,0,128),(6,3,0,128,128),(7,4,0,0,96),(7,4,0,96,80)]
+NC = len(CH)
+BUF = [(1024,1024),(256,1024),(1024,704),(1024,704),(704,1024)]
+LA = 2
+def split(rows):
+    q = rows//4
+    h = (q//2 + 15)//16*16
+    return q, h
+
+def gather_kernel(order, *refs):
+    ins = refs[:8]; outs = refs[8:13]; bufs = refs[13:18]; zs, zr, xs, xr, ys, yr, fs, fr, fzs, loc = refs[18:]
+    dp = lax.axis_index("dp"); z = lax.axis_index("mp")
+    c = dp % 2; bx = (dp//2)%2; by = (dp//4)%2; p = by*2+bx
+    xn = dp + 2 - 4*bx; yn = dp + 4 - 8*by
+    px = by*2 + 1-bx; py = (1-by)*2 + bx; pd = (1-by)*2 + 1-bx
+    bar = pltpu.get_barrier_semaphore()
+    base = dp - 2*p
+    peers = []
+    for k in range(4):
+        for zz in range(4):
+            pl.semaphore_signal(bar, inc=1, device_id=(base+2*k, zz), device_id_type=MESH)
+    pl.semaphore_wait(bar, 16)
+    innet = z//2 == c
+    own = z % 2
+    def sl(ref, j, ch, row, rows):
+        i, b, co, _, _ = ch
+        cols = W[i][1]
+        if BUF[b][1] == cols: return bufs[b].at[j, pl.ds(pl.multiple_of(row,16), rows), :]
+        return bufs[b].at[j, pl.ds(pl.multiple_of(row,16), rows), pl.ds(co, cols)]
+    def rc(src, dst, s, r, d): return pltpu.make_async_remote_copy(src, dst, s, r, device_id=d, device_id_type=MESH)
+    def part(ch, who):
+        q = W[ch[0]][0]//4
+        h = (ch[4]//2+15)//16*16
+        return who*q + ch[3], ch[4], h
+    def zsrc(k, d):
+        ch = CH[k]; r0, n, h = part(ch, p)
+        return rc(ins[ch[0]].at[pl.ds(pl.multiple_of(r0,16), n), :], sl(None, own, ch, r0, n), zs.at[k, d], zr.at[k, own], (dp, z+1-2*d))
+    def zfwd(k, j, d):
+        ch = CH[k]; r0, n, h = part(ch, p); r = sl(None, j, ch, r0, n)
+        return rc(r, r, fzs.at[k, j], zr.at[k, j], (dp, z+1-2*d))
+    @pl.when(innet)
+    def _():
+        for k in range(NC):
+            @pl.when(z<3)
+            def _(): zsrc(k, 0).start()
+            @pl.when(z>0)
+            def _(): zsrc(k, 1).start()
+        for i, (b, co) in enumerate([(0,0),(0,256),(0,512),(0,768),(1,0),(2,0),(3,0),(4,0)]):
+            dst = bufs[b].at[own] if b else bufs[b].at[own, :, pl.ds(co,256)]
+            pltpu.make_async_copy(ins[i], dst, loc.at[i]).start()
+    def xdesc(k, j):
+        ch = CH[k]; r0, n, h = part(ch, p); r = sl(None, j, ch, r0, n)
+        return rc(r, r, xs.at[k,j], xr.at[k,j], (xn, z))
+    def ydesc(k, j):
+        ch = CH[k]; r0, n, h = part(ch, p); r = sl(None, j, ch, r0, n)
+        return rc(r, r, ys.at[k,j], yr.at[k,j], (yn, z))
+    def fdesc0(k, j):
+        ch = CH[k]; r0, n, h = part(ch, px); r = sl(None, j, ch, r0, h)
+        return rc(r, r, fs.at[0,k,j], fr.at[0,k,j], (yn, z))
+    def fdesc1(k, j):
+        ch = CH[k]; r0, n, h = part(ch, py); r = sl(None, j, ch, r0+h, n-h)
+        return rc(r, r, fs.at[1,k,j], fr.at[1,k,j], (xn, z))
+    def A(k, j):
+        s = 2*c + j
+        zfwd(k, j, 0).wait_recv()
+        @pl.when((z > s) & (z < 3))
+        def _(): zfwd(k, j, 0).start()
+        @pl.when((z < s) & (z > 0))
+        def _(): zfwd(k, j, 1).start()
+        xdesc(k, j).start(); ydesc(k, j).start()
+    def B(k, j):
+        xdesc(k, j).wait_recv(); fdesc0(k, j).start()
+        ydesc(k, j).wait_recv(); fdesc1(k, j).start()
+    def C(k, j):
+        fdesc0(k, j).wait_recv(); fdesc1(k, j).wait_recv()
+    j0 = jnp.where(innet, 1-own, 1-c)
+    def steps(F, k):
+        F(k, j0)
+        @pl.when(jnp.logical_not(innet))
+        def _(): F(k, 1-j0)
+    for t in range(NC+2*LA):
+        if t < NC: steps(A, t)
+        if 0 <= t-LA < NC: steps(B, t-LA)
+        if 0 <= t-2*LA < NC: steps(C, t-2*LA)
+    @pl.when(innet)
+    def _():
+        for k in range(NC):
+            @pl.when(z<3)
+            def _(): zsrc(k, 0).wait_send()
+            @pl.when(z>0)
+            def _(): zsrc(k, 1).wait_send()
+        for i, (b, co) in enumerate([(0,0),(0,256),(0,512),(0,768),(1,0),(2,0),(3,0),(4,0)]):
+            dst = bufs[b].at[own] if b else bufs[b].at[own, :, pl.ds(co,256)]
+            pltpu.make_async_copy(ins[i], dst, loc.at[i]).wait()
+    def D(k, j):
+        s = 2*c + j
+        @pl.when(((z > s) & (z < 3)) | ((z < s) & (z > 0)))
+        def _(): zfwd(k, j, 0).wait_send()
+        xdesc(k, j).wait_send(); ydesc(k,j).wait_send(); fdesc0(k,j).wait_send(); fdesc1(k,j).wait_send()
+    for k in range(NC): steps(D, k)
+    for b in range(5):
+        pltpu.make_async_copy(bufs[b], outs[b], loc.at[b]).start()
+    for b in range(5):
+        pltpu.make_async_copy(bufs[b], outs[b], loc.at[b]).wait()
+
+def ring_weights(*ins):
+    return pl.pallas_call(functools.partial(gather_kernel, None),
+        out_shape=[jax.ShapeDtypeStruct((2,)+s, jnp.bfloat16) for s in BUF],
+        in_specs=[pl.BlockSpec(memory_space=pl.ANY)]*8, out_specs=[pl.BlockSpec(memory_space=pl.ANY)]*5,
+        scratch_shapes=[pltpu.VMEM((2,)+s, jnp.bfloat16) for s in BUF] + [pltpu.SemaphoreType.DMA((NC,2)), pltpu.SemaphoreType.DMA((NC,2))] + [pltpu.SemaphoreType.DMA((NC,2))]*4 + [pltpu.SemaphoreType.DMA((2,NC,2))]*2 + [pltpu.SemaphoreType.DMA((NC,2)), pltpu.SemaphoreType.DMA((8,))],
+        compiler_params=pltpu.CompilerParams(collective_id=0, has_side_effects=True, vmem_limit_bytes=60*2**20), name="ag")(*ins)
+
+
 def gather_weight(weight):
     rows = weight.shape[0] // lax.axis_size("dp")
     part = lax.dynamic_slice_in_dim(weight, lax.axis_index("dp") * rows, rows, 0)
@@ -74,11 +193,18 @@
     low = jnp.bfloat16
     parts = lax.axis_size("mp")
     heads_wide = w_query.shape[1]
-    w_in = gather_weight(jnp.concatenate([w_query, w_key, w_value, w_gate], axis=1))
-    full_out = gather_weight(w_out).reshape(-1, w_out.shape[1])
-    full_first = gather_weight(w_first)
-    full_second = gather_weight(w_second)
-    full_third = gather_weight(w_third).reshape(-1, w_third.shape[1])
+    mine = ring_weights(w_query, w_key, w_value, w_gate, w_out, w_first, w_second, w_third)
+    count = lax.axis_size("dp")
+    pairs = [(i, i + 1 - 2 * (i % 2)) for i in range(count)]
+    first = lax.axis_index("dp") % 2 == 0
+
+    def both(array):
+        other = lax.ppermute(array, "dp", pairs)
+        return jnp.concatenate([jnp.where(first, array, other), jnp.where(first, other, array)])
+
+    w_in, full_out, full_first, full_second, full_third = [both(m) for m in mine]
+    full_out = full_out.reshape(-1, w_out.shape[1])
+    full_third = full_third.reshape(-1, w_third.shape[1])
     gain = lax.all_gather(head_gain, "mp", axis=0, tiled=True)
 
     residual = inputs.astype(jnp.float32)

time: 1190 us -> 1070 us (0.90)
  waiting for transfers between devices: 806 us -> 532 us
  Pallas kernels: 0 us -> 62.7 us
  starting transfers between devices: 0.58 us -> 47.8 us
  local copies, waits for them, and re-layouts: 122 us -> 160 us
  other arithmetic: 47.7 us -> 68.6 us
    all_gather x5 -> x0, waiting for transfers between devices: 253 us -> none  [gather_weight(): full = lax.all_gather(part, ALL, axis=0, tiled=True)]
    pallas_call x0 -> x1, Pallas kernels: none -> 62.7 us  [ring_weights(): pl.pallas_call(functools.partial(gather_kernel, None), out_shape=[jax.Sha...]
    ppermute x0 -> x5, starting transfers between devices: none -> 46.8 us  [both(): other = lax.ppermute(array, 'dp', pairs)]
    unnamed x16 -> x11, waiting for transfers between devices: 95.9 us -> 63.5 us
    select_n x0 -> x5, other arithmetic: none -> 14 us  [both(): jnp.where(first, array, other)]
    unnamed x140 -> x198, local copies, waits for them, and re-layouts: 27.3 us -> 39.4 us
  transfers between devices with their start and end apart: 14 -> 14, of which waited for: 12 -> 9; matrix products, arithmetic and copies ran while one was open for 22% -> 21% of each run, Pallas kernels for 0% -> 0%
where the time goes in v2:
time: 1070 us
  waiting for transfers between devices  532 us (50%)
  local copies, waits for them, and re-layouts  160 us (15%)
  matrix products  127 us (12%)
  other arithmetic  68.6 us (6%)
  Pallas kernels  62.7 us (6%)
  blocking collectives  53.9 us (5%)
  starting transfers between devices  47.8 us (4%)
  between operations  15.5 us (1%)
    reduce_scatter x3, waiting for transfers between devices, reduce_gradient(): lax.psum_scatter(stacked.reshape(shards_ * rows, columns), ALL, scatter_d...  372 us
    all_gather x4, waiting for transfers between devices, reduce_gradient(): return lax.all_gather(part, 'dp', axis=0, tiled=True)  88.1 us
    unnamed x11, waiting for transfers between devices  63.5 us
    pallas_call x1, Pallas kernels, ring_weights(): pl.pallas_call(functools.partial(gather_kernel, None), out_shape=[jax.Sha...  62.7 us
    ppermute x5, starting transfers between devices, both(): other = lax.ppermute(array, 'dp', pairs)  46.8 us
    dot_general x14, matrix products, matmul_nt(): lax.dot_general(left, right, (((1,), (1,)), ((), ())), preferred_element_...  46.4 us
    unnamed x198, local copies, waits for them, and re-layouts  39.4 us
    psum x1, blocking collectives, shards(): grad_head_gain = lax.psum(grad_head_gain, ALL)  37.2 us
  transfers between devices with their start and end apart: 14, of which 9 were waited for; matrix products, arithmetic and copies ran while one was open for 21% of the time, Pallas kernels for 0%

profile of v2, /device:TPU:0, one launch (start us, length us, event | category | flops | bytes accessed | tf_op | source)
XLA Modules:
  0.0 1067.2 jit_solution(3092755488673431408)
XLA Ops:
  11.4 62.7 %ag.1 = (bf16[2,1024,1024]{2,1,0:T(8,128)(2,1)}, bf16[2,256,1024]{2,1,0:T(8,128)(2,1)}, bf16[2,1024,704]{2,1,0:T(8,128)(2,1)}, bf16[2,1024,704]{2,1,0:T(8,128)(2,1)}, bf16[2,704,1024]{2,1,0:T(8,128)(2,1)}) custom-call(bf16[1024,256]{1,0:T(8,128)(2,1)} %refs_0_.1, bf16[1024,256]{1,0:T(8,128)(2,1)} %refs_1_.1, bf16[1024,256]{1,0:T(8,128)(2,1)} %refs_2_.1, ...), custom_call_target="tpu_custom_call" | custom-call | tf_op jit(solution)/shard_map/ag/pallas_call | solution.py:170
  74.2 4.7 copy.87
  78.9 45.8 %collective-permute-start.3 = (bf16[2,1024,704]{1,2,0:T(8,128)(2,1)}, bf16[2,1024,704]{1,2,0:T(8,128)(2,1)}, u32[]{:S(2)}, u32[]{:S(2)}) collective-permute-start(bf16[2,1024,704]{1,2,0:T(8,128)(2,1)} %copy.87), channel_id=1, source_target_pairs={{0,4},{4,0},{8,12},{12,8},{16,20},{20,16},{24,28},{28,24},{1,5},{5... | collective-permute-start | bytes 8650760 | tf_op jit(solution)/shard_map/ppermute | solution.py:202
  128.4 7.6 all-gather
  137.6 8.1 collective-permute-done.1
  148.9 4.8 copy.88
  153.7 4.6 copy.85
  161.4 3.4 pad_maximum_fusion.3
  166.3 3.1 broadcast_select_fusion.3
  169.5 3.5 broadcast_select_fusion.5
  193.6 3.2 copy.99
  196.8 4.0 convert_element_type.155
  200.8 3.7 copy.103
  204.5 3.6 pad_maximum_fusion.6
  208.1 4.7 concatenate.45
  212.8 5.5 copy.82
  218.4 5.4 fusion.105
  223.8 4.2 multiply_reduce_fusion.1
  232.5 3.6 copy.83
  238.9 3.3 multiply_reduce_fusion.5
  261.9 9.2 fusion.1
  276.7 3.1 pad_maximum_fusion.4
  279.8 8.4 copy.122
  293.3 3.2 pad_maximum_fusion.5
  296.5 8.6 copy.123
  305.2 6.0 copy.91
  311.1 7.7 copy.94
  321.1 5.0 reshape.135
  326.0 4.9 reshape.137
  331.0 3.7 fusion.41
  334.6 3.6 fusion.39
  338.2 3.7 fusion.37
  341.9 3.7 fusion.50
  345.6 5.0 convolution_convert_fusion
  351.1 3.2 fusion.48
  359.1 5.5 multiply_reduce_fusion.4
  382.9 5.2 multiply_convert_fusion.7
  388.1 4.0 reshape.138
  392.1 4.5 copy.107
  396.6 5.4 convert_bitcast_fusion.4
  402.0 4.4 copy.109
  406.4 4.1 convert_element_type.176
  410.5 5.0 multiply_reduce_fusion
  421.3 4.3 convert_element_type.170
  425.6 3.6 fusion.28
  431.9 4.1 convert_element_type.173
  445.7 3.8 pad_maximum_fusion
  449.5 5.2 convolution_convert_fusion.1
  457.1 63.3 %reduce-scatter.18.cloned.1.call-done = bf16[128,704]{1,0:T(8,128)(2,1)} async-done(((bf16[4096,704]{1,0:T(8,128)(2,1)}), bf16[128,704]{1,0:T(8,128)(2,1)}) %reduce-scatter.18.cloned.1.call-update) | async-done | bytes 180240
  522.3 143.7 %reduce-scatter.14.cloned.1.call-done = bf16[88,1024]{1,0:T(8,128)(2,1)} async-done(((bf16[2816,1024]{1,0:T(8,128)(2,1)}), bf16[88,1024]{1,0:T(8,128)(2,1)}) %reduce-scatter.14.cloned.1.call-update) | async-done | bytes 180240 | tf_op jit(solution)/shard_map/reduce_scatter | solution.py:186
  666.1 147.0 %reduce-scatter.10.cloned.1.call-done = bf16[128,1024]{1,0:T(8,128)(2,1)} async-done(((bf16[4096,1024]{1,0:T(8,128)(2,1)}), bf16[128,1024]{1,0:T(8,128)(2,1)}) %reduce-scatter.10.cloned.1.call-update) | async-done | bytes 262160 | tf_op jit(solution)/shard_map/reduce_scatter | solution.py:186
  813.1 37.2 %psum.7 = f32[1024]{0:T(1024)S(1)} all-reduce(f32[1024]{0:T(1024)S(1)} %get-tuple-element.21), channel_id=1, replica_groups=mesh['dp'=8,'mp'=4] {'mp','dp'}, use_global_device_ids=true, to_apply=%region_11.12 | all-reduce | flops 1024 | bytes 8192 | tf_op jit(solution)/shard_map/psum | solution.py:309
  850.9 3.2 fusion.20
  862.6 4.5 convolution_add_fusion
  867.1 81.3 %reduce-scatter.12.cloned.1.call-done = bf16[32,1024]{1,0:T(8,128)(2,1)} async-done(((bf16[1024,1024]{1,0:T(8,128)(2,1)}), bf16[32,1024]{1,0:T(8,128)(2,1)}) %reduce-scatter.12.cloned.1.call-update) | async-done | bytes 65552 | tf_op jit(solution)/shard_map/reduce_scatter | solution.py:186
  948.4 9.2 all_gather.20
  958.6 13.4 %all-gather.8.cloned.1.call-done = bf16[1024,704]{0,1:T(8,128)(2,1)} async-done(((bf16[128,704]{0,1:T(8,128)(2,1)}), bf16[1024,704]{0,1:T(8,128)(2,1)}) %all-gather.8.cloned.1.call-update) | async-done | bytes 1441808 | tf_op jit(solution)/shard_map/all_gather | solution.py:187
  972.0 3.3 convert_element_type.193
  975.3 24.1 %all-gather.10.cloned.1.call-done = bf16[1024,704]{0,1:T(8,128)(2,1)} async-done(((bf16[128,704]{0,1:T(8,128)(2,1)}), bf16[1024,704]{0,1:T(8,128)(2,1)}) %all-gather.10.cloned.1.call-update) | async-done | bytes 1441808 | tf_op jit(solution)/shard_map/all_gather | solution.py:187
  999.4 3.3 convert_element_type.198
  1002.7 23.9 %all-gather.12.cloned.1.call-done = bf16[704,1024]{1,0:T(8,128)(2,1)} async-done(((bf16[88,1024]{1,0:T(8,128)(2,1)}), bf16[704,1024]{1,0:T(8,128)(2,1)}) %all-gather.12.cloned.1.call-update) | async-done | bytes 1441808 | tf_op jit(solution)/shard_map/all_gather | solution.py:187
  1026.6 3.3 convert_element_type.200
  1029.9 26.7 %all-gather.6.cloned.1.call-done = bf16[1024,1024]{1,0:T(8,128)(2,1)} async-done(((bf16[128,1024]{1,0:T(8,128)(2,1)}), bf16[1024,1024]{1,0:T(8,128)(2,1)}) %all-gather.6.cloned.1.call-update) | async-done | bytes 2097168 | tf_op jit(solution)/shard_map/all_gather | solution.py:187
  1056.6 3.6 slice_convert_fusion
  (306 shorter events, 133.0 us)
Async XLA Ops:
  7.2 447.7 %reduce-scatter.16.cloned.1.call-start = ((), (), s32[]{:S(2)}) async-start(), calls=%async_computation.12 | async-start | bytes 6488064
  74.1 50.5 %copy-start.5 = (bf16[2,1024,704]{2,1,0:T(8,128)(2,1)S(1)}, bf16[2,1024,704]{2,1,0:T(8,128)(2,1)}, u32[]{:S(2)}) copy-start(bf16[2,1024,704]{2,1,0:T(8,128)(2,1)} %get-tuple-element.18) | copy-start | bytes 8650756
  78.9 70.0 %collective-permute-start.3 = (bf16[2,1024,704]{1,2,0:T(8,128)(2,1)}, bf16[2,1024,704]{1,2,0:T(8,128)(2,1)}, u32[]{:S(2)}, u32[]{:S(2)}) collective-permute-start(bf16[2,1024,704]{1,2,0:T(8,128)(2,1)} %copy.87), channel_id=1, source_target_pairs={{0,4},{4,0},{8,12},{12,8},{16,20},{20,16},{24,28},{28,24},{1,5},{5... | collective-permute-start | bytes 8650760 | tf_op jit(solution)/shard_map/ppermute | solution.py:202
  124.6 3.7 copy-start.90
  127.3 26.4 %collective-permute-start.2 = (bf16[2,1024,704]{1,2,0:T(8,128)(2,1)}, bf16[2,1024,704]{1,2,0:T(8,128)(2,1)}, u32[]{:S(2)}, u32[]{:S(2)}) collective-permute-start(bf16[2,1024,704]{1,2,0:T(8,128)(2,1)} %copy.84), channel_id=1, source_target_pairs={{0,4},{4,0},{8,12},{12,8},{16,20},{20,16},{24,28},{28,24},{1,5},{5... | collective-permute-start | bytes 8650760 | tf_op jit(solution)/shard_map/ppermute | solution.py:202
  127.3 31.0 %collective-permute-start.4 = (bf16[2,704,1024]{2,1,0:T(8,128)(2,1)}, bf16[2,704,1024]{2,1,0:T(8,128)(2,1)}, u32[]{:S(2)}, u32[]{:S(2)}) collective-permute-start(bf16[2,704,1024]{2,1,0:T(8,128)(2,1)} %get-tuple-element.20), channel_id=1, source_target_pairs={{0,4},{4,0},{8,12},{12,8},{16,20},{20,16},{24,28},{28,24},{1,5},{5... | collective-permute-start | bytes 8650760 | tf_op jit(solution)/shard_map/ppermute | solution.py:202
  127.8 45.2 %collective-permute-start = (bf16[2,1024,1024]{2,1,0:T(8,128)(2,1)}, bf16[2,1024,1024]{2,1,0:T(8,128)(2,1)}, u32[]{:S(2)}, u32[]{:S(2)}) collective-permute-start(bf16[2,1024,1024]{2,1,0:T(8,128)(2,1)} %get-tuple-element.16), channel_id=1, source_target_pairs={{0,4},{4,0},{8,12},{12,8},{16,20},{20,16},{24,28},{28,24},{1,5},{5... | collective-permute-start | bytes 12582920 | tf_op jit(solution)/shard_map/ppermute | solution.py:202
  127.9 17.8 %collective-permute-start.1 = (bf16[2,256,1024]{2,1,0:T(8,128)(2,1)}, bf16[2,256,1024]{2,1,0:T(8,128)(2,1)}, u32[]{:S(2)}, u32[]{:S(2)}) collective-permute-start(bf16[2,256,1024]{2,1,0:T(8,128)(2,1)} %get-tuple-element.17), channel_id=1, source_target_pairs={{0,4},{4,0},{8,12},{12,8},{16,20},{20,16},{24,28},{28,24},{1,5},{5... | collective-permute-start | bytes 3145736 | tf_op jit(solution)/shard_map/ppermute | solution.py:202
  135.9 11.4 %copy-start.86 = (f32[4,1,256]{2,1,0:T(1,128)}, f32[4,1,256]{2,1,0:T(1,128)S(1)}, u32[]{:S(2)}) copy-start(f32[4,1,256]{2,1,0:T(1,128)S(1)} %all-gather) | copy-start | bytes 12292
  137.5 42.7 %copy-start.88 = (f32[512]{0:T(512)}, f32[512]{0:T(512)S(1)}, u32[]{:S(2)}) copy-start(f32[512]{0:T(512)S(1)} %add_rsqrt_fusion.2) | copy-start | bytes 6148
  161.4 3.4 copy-start.6
  161.4 4.9 copy-start.7
  166.3 3.2 copy-start.8
  169.5 3.5 copy-start.30
  175.6 4.6 copy-start.26
  181.7 22.8 %copy-start.20 = (f32[512,256]{1,0:T(8,128)}, f32[512,256]{1,0:T(8,128)S(1)}, u32[]{:S(2)}) copy-start(f32[512,256]{1,0:T(8,128)S(1)} %slice.273) | copy-start | bytes 1572868
  182.6 21.9 %copy-start.22 = (f32[512,256]{1,0:T(8,128)}, f32[512,256]{1,0:T(8,128)S(1)}, u32[]{:S(2)}) copy-start(f32[512,256]{1,0:T(8,128)S(1)} %slice.272) | copy-start | bytes 1572868
  204.5 13.9 %copy-start.11 = (bf16[8,64,16,64]{1,3,2,0:T(8,128)(2,1)}, bf16[8,64,16,64]{1,3,2,0:T(8,128)(2,1)S(1)}, u32[]{:S(2)}) copy-start(bf16[8,64,16,64]{1,3,2,0:T(8,128)(2,1)S(1)} %copy.103) | copy-start | bytes 3145732
  223.8 6.2 copy-start.4
  242.2 5.1 copy-start.1
  242.2 3.0 copy-start.42
  242.4 17.5 %copy-start.52 = (bf16[512,1024]{1,0:T(8,128)(2,1)}, bf16[512,1024]{1,0:T(8,128)(2,1)S(1)}, u32[]{:S(2)}) copy-start(bf16[512,1024]{1,0:T(8,128)(2,1)S(1)} %multiply_convert_fusion.8) | copy-start | bytes 3145732
  253.6 4.2 copy-start.44
  255.7 6.2 slice-start
  257.8 4.1 slice-start.1
  288.3 232.2 %reduce-scatter.18.cloned.1.call-start = ((), (), s32[]{:S(2)}) async-start(), calls=%async_computation.13 | async-start | bytes 6488064
  305.1 360.9 %reduce-scatter.14.cloned.1.call-start = ((), (), s32[]{:S(2)}) async-start(), calls=%async_computation.10 | async-start | bytes 5947392 | tf_op jit(solution)/shard_map/reduce_scatter | solution.py:186
  326.0 4.9 copy-start.16
  331.0 3.7 copy-start.45
  338.2 3.7 copy-start.43
  341.9 3.7 copy-start.18
  341.9 3.7 copy-start.50
  350.6 3.6 copy-start.40
  350.6 462.4 %reduce-scatter.10.cloned.1.call-start = ((), (), s32[]{:S(2)}) async-start(), calls=%async_computation.5 | async-start | bytes 8650752 | tf_op jit(solution)/shard_map/reduce_scatter | solution.py:186
  351.1 5.5 copy-start.41
  354.3 4.7 copy-start.17
  359.1 5.5 copy-start.51
  359.1 6.1 copy-start.48
  364.6 3.0 copy-start.46
  410.5 5.0 copy-start.38
  437.7 3.7 copy-start.69
  437.7 5.1 copy-start.63
  437.7 6.5 copy-start.59
  438.0 3.3 copy-start.75
  438.0 4.8 copy-start.71
  438.0 6.2 copy-start.65
  439.7 3.1 copy-start.77
  439.7 4.6 copy-start.73
  439.8 3.0 copy-start.82
  439.8 4.5 copy-start.79
  449.5 498.9 %reduce-scatter.12.cloned.1.call-start = ((), (), s32[]{:S(2)}) async-start(), calls=%async_computation.7 | async-start | bytes 2162688 | tf_op jit(solution)/shard_map/reduce_scatter | solution.py:186
  454.8 396.1 %copy-start.70 = (bf16[512,256]{1,0:T(8,128)(2,1)S(1)}, bf16[512,256]{1,0:T(8,128)(2,1)}, u32[]{:S(2)}) copy-start(bf16[512,256]{1,0:T(8,128)(2,1)} %copy-done.69) | copy-start | bytes 786436
  454.8 396.1 %copy-start.76 = (bf16[512,256]{1,0:T(8,128)(2,1)S(1)}, bf16[512,256]{1,0:T(8,128)(2,1)}, u32[]{:S(2)}) copy-start(bf16[512,256]{1,0:T(8,128)(2,1)} %copy-done.75) | copy-start | bytes 786436
  454.8 517.2 %all-gather.8.cloned.1.call-start = ((), (), s32[]{:S(2)}) async-start(), calls=%async_computation.8 | async-start | bytes 1622016 | tf_op jit(solution)/shard_map/all_gather | solution.py:187
  456.8 542.5 %all-gather.10.cloned.1.call-start = ((), (), s32[]{:S(2)}) async-start(), calls=%async_computation.9 | async-start | bytes 1622016 | tf_op jit(solution)/shard_map/all_gather | solution.py:187
  522.2 504.4 %all-gather.12.cloned.1.call-start = ((), (), s32[]{:S(2)}) async-start(), calls=%async_computation.11 | async-start | bytes 1622016 | tf_op jit(solution)/shard_map/all_gather | solution.py:187
  666.0 390.6 %all-gather.6.cloned.1.call-start = ((), (), s32[]{:S(2)}) async-start(), calls=%async_computation.6 | async-start | bytes 2359296 | tf_op jit(solution)/shard_map/all_gather | solution.py:187
  850.9 3.2 copy-start.29
  850.9 3.2 copy-start.64
  850.9 3.3 copy-start.72
  850.9 3.3 copy-start.78
  850.9 3.3 copy-start.83
  855.6 6.1 slice-start.2
  858.0 3.7 slice-start.3
  (46 other events, 94.6 us)
Sparse Core Ops, SparseCore 0:
  288.4 111.5 reduce-scatter.15
  406.6 113.8 reduce-scatter.17
  522.8 143.2 reduce-scatter.13
  668.1 144.8 reduce-scatter.9
  815.7 132.5 reduce-scatter.11
  950.8 21.1 all-gather.7
  974.0 25.2 all-gather.9
  1001.4 25.1 all-gather.11
  1028.6 27.8 all-gather.5

commit v3 on v1

v3 whole, which is shorter than its diff:
```python
import functools

import jax
import jax.numpy as jnp
from jax import lax
from jax.experimental import pallas as pl
from jax.experimental.pallas import tpu as pltpu
from jax.sharding import PartitionSpec as P

DH = 64
BLK = 64
EPSILON = 1e-06
MESH = pl.DeviceIdType.MESH
F32 = jnp.float32
BF16 = jnp.bfloat16
UNIT = 128
VMEM_LIMIT = 60 * 2**20


def rms_factor(values):
    return lax.rsqrt(jnp.mean(values * values, axis=-1, keepdims=True) + EPSILON)


def dot(left, right):
    return jnp.dot(left, right, preferred_element_type=F32)


def dot_tn(left, right):
    return lax.dot_general(left, right, (((0,), (0,)), ((), ())), preferred_element_type=F32)


def dot_nt(left, right):
    return lax.dot_general(left, right, (((1,), (1,)), ((), ())), preferred_element_type=F32)


def remote(src, dst, send, recv, device):
    return pltpu.make_async_remote_copy(src, dst, send, recv, device_id=device, device_id_type=MESH)


def rows_of(start, count):
    return pl.ds(pl.multiple_of(start, 16), count)


class Place:
    def __init__(self):
        dp, self.z = lax.axis_index("dp"), lax.axis_index("mp")
        self.dp = dp
        self.c = dp % 2
        self.bx, self.by = (dp // 2) % 2, (dp // 4) % 2
        self.p = self.by * 2 + self.bx
        self.px, self.py = self.by * 2 + 1 - self.bx, (1 - self.by) * 2 + self.bx
        self.pd = (1 - self.by) * 2 + 1 - self.bx
        self.sib = (dp + 1 - 2 * self.c, self.z)
        self.xn = (dp + 2 - 4 * self.bx, self.z)
        self.yn = (dp + 4 - 8 * self.by, self.z)
        self.own = self.z % 2
        self.innet = self.z // 2 == self.c

    def up(self):
        return (self.dp, self.z + 1)

    def down(self):
        return (self.dp, self.z - 1)


def half_of(count):
    return (count // 2 + 15) // 16 * 16


def gather_plan(shapes):
    plan = []
    for i, (rows, _) in enumerate(shapes):
        quarter = rows // 4
        if i < 4:
            parts = [quarter]
        elif i == 4:
            parts = [quarter]
        else:
            first = half_of(quarter)
            parts = [first, quarter - first]
        start = 0
        for count in parts:
            plan.append((i, max(i - 3, 0), i * shapes[0][1] if i < 4 else 0, start, count))
            start += count
    return plan


def forward_kernel(plan, shapes, *refs):
    nw = 8
    x_in, cot_in, gain_in = refs[:3]
    w_in = refs[3 : 3 + nw]
    outs = refs[3 + nw : 3 + nw + 18]
    (w_out, a_out, qkv_out, u_out, o_out, p_out, z_out, h_out, b_out, m_out, d1_out, d2_out, cot_out, gain_out) = (
        outs[:5], *outs[5:]
    )
    scratch = refs[3 + nw + 18 :]
    bufs = scratch[:5]
    (x_ref, cot, a_ref, qkv, u_ref, o_ref, p_ref, z_ref, hs, hr, h_ref, b_ref, m_ref, d1, d2, gain) = scratch[5:21]
    (zs, zr, fzs, xs, xr, ys, yr, fs, fr, loc, gs, gr, es, er, sv) = scratch[21:]
    me = Place()
    z, c, own, innet = me.z, me.c, me.own, me.innet
    T = x_in.shape[0]
    TT = 2 * T
    count = len(plan)
    wide = shapes[0][1]

    bar = pltpu.get_barrier_semaphore()
    for d in (me.sib, me.xn, me.yn):
        pl.semaphore_signal(bar, inc=1, device_id=d, device_id_type=MESH)

    @pl.when(z < 3)
    def _():
        pl.semaphore_signal(bar, inc=1, device_id=me.up(), device_id_type=MESH)

    @pl.when(z > 0)
    def _():
        pl.semaphore_signal(bar, inc=1, device_id=me.down(), device_id_type=MESH)

    pl.semaphore_wait(bar, 3 + jnp.where(z < 3, 1, 0) + jnp.where(z > 0, 1, 0))

    def piece(k, who):
        i, _, _, start, rows = plan[k]
        return who * (shapes[i][0] // 4) + start, rows

    def part(j, k, row, rows):
        _, buf, col, _, _ = plan[k]
        ref = bufs[buf]
        if buf:
            return ref.at[j, rows_of(row, rows), :]
        return ref.at[j, rows_of(row, rows), pl.ds(col, wide)]

    def z_first(k, d):
        row, rows = piece(k, me.p)
        src = w_in[plan[k][0]].at[rows_of(row, rows), :]
        return remote(src, part(own, k, row, rows), zs.at[k, d], zr.at[k, own], (me.dp, z + 1 - 2 * d))

    def z_next(k, j, d):
        row, rows = piece(k, me.p)
        r = part(j, k, row, rows)
        return remote(r, r, fzs.at[k, j], zr.at[k, j], (me.dp, z + 1 - 2 * d))

    def to_x(k, j):
        row, rows = piece(k, me.p)
        r = part(j, k, row, rows)
        return remote(r, r, xs.at[k, j], xr.at[k, j], me.xn)

    def to_y(k, j):
        row, rows = piece(k, me.p)
        r = part(j, k, row, rows)
        return remote(r, r, ys.at[k, j], yr.at[k, j], me.yn)

    def x_then_y(k, j):
        row, rows = piece(k, me.px)
        r = part(j, k, row, half_of(rows))
        return remote(r, r, fs.at[0, k, j], fr.at[0, k, j], me.yn)

    def y_then_x(k, j):
        row, rows = piece(k, me.py)
        h = half_of(rows)
        r = part(j, k, row + h, rows - h)
        return remote(r, r, fs.at[1, k, j], fr.at[1, k, j], me.xn)

    def gain_copy(j, d, src):
        return remote(src, gain.at[j], gs.at[j, d], gr.at[j], (me.dp, z + 1 - 2 * d))

    def own_copies():
        copies = []
        for i in range(nw):
            dst = bufs[i - 3].at[own] if i > 3 else bufs[0].at[own, :, pl.ds(i * wide, wide)]
            copies.append(pltpu.make_async_copy(w_in[i], dst, loc.at[i]))
        copies.append(pltpu.make_async_copy(gain_in, gain.at[own], loc.at[nw]))
        return copies

    both = [
        remote(x_in, x_ref.at[pl.ds(T, T), :], es.at[0], er.at[0], me.sib),
        remote(cot_in, cot.at[pl.ds(T, T), :], es.at[1], er.at[1], me.sib),
    ]
    mine = [
        pltpu.make_async_copy(x_in, x_ref.at[pl.ds(0, T), :], loc.at[nw + 1]),
        pltpu.make_async_copy(cot_in, cot.at[pl.ds(0, T), :], loc.at[nw + 2]),
    ]
    mine[0].start()
    both[0].start()

    @pl.when(innet)
    def _():
        @pl.when(z < 3)
        def _():
            gain_copy(own, 0, gain_in).start()

        @pl.when(z > 0)
        def _():
            gain_copy(own, 1, gain_in).start()

        for k in range(count):
            @pl.when(z < 3)
            def _():
                z_first(k, 0).start()

            @pl.when(z > 0)
            def _():
                z_first(k, 1).start()

        for copy in own_copies():
            copy.start()

    mine[1].start()
    both[1].start()

    def upward(j):
        return (z > 2 * c + j) & (z < 3)

    def downward(j):
        return (z < 2 * c + j) & (z > 0)

    def others(step, *args):
        for j in (0, 1):
            @pl.when(z != 2 * c + j)
            def _():
                step(*args, j)

    def step_gain(j):
        gain_copy(j, 0, gain.at[j]).wait_recv()

        @pl.when(upward(j))
        def _():
            gain_copy(j, 0, gain.at[j]).start()

        @pl.when(downward(j))
        def _():
            gain_copy(j, 1, gain.at[j]).start()

    def step_a(k, j):
        z_next(k, j, 0).wait_recv()

        @pl.when(upward(j))
        def _():
            z_next(k, j, 0).start()

        @pl.when(downward(j))
        def _():
            z_next(k, j, 1).start()

        to_x(k, j).start()
        to_y(k, j).start()

    def step_b(k, j):
        to_x(k, j).wait_recv()
        x_then_y(k, j).start()
        to_y(k, j).wait_recv()
        y_then_x(k, j).start()

    def step_c(k, j):
        x_then_y(k, j).wait_recv()
        y_then_x(k, j).wait_recv()

    ahead = 2
    steps = []
    for t in range(count + 2 * ahead):
        for step, lag in ((step_a, 0), (step_b, ahead), (step_c, 2 * ahead)):
            if 0 <= t - lag < count:
                steps.append((step, t - lag))
    done = [0]

    def pump(until=None, number=0):
        while done[0] < len(steps) and (number > 0 or until is not None):
            step, k = steps[done[0]]
            others(step, k)
            done[0] += 1
            number -= 1
            if step is step_c and until is not None and k >= until:
                until = None

    saves = []

    def save(src, dst):
        copy = pltpu.make_async_copy(src, dst, sv.at[len(saves)])
        copy.start()
        saves.append(copy)

    mine[0].wait()
    both[0].wait_recv()

    def norm_rows(t, carry):
        rows = rows_of(t * UNIT, UNIT)
        values = x_ref[rows, :].astype(F32)
        a_ref[rows, :] = (values * rms_factor(values)).astype(BF16)
        return carry

    lax.fori_loop(0, TT // UNIT, norm_rows, 0)
    save(a_ref, a_out)

    @pl.when(innet)
    def _():
        for copy in own_copies():
            copy.wait()

    others(step_gain)

    lane = lax.broadcasted_iota(jnp.int32, (UNIT, UNIT), 1)
    low_half = lane < DH
    keep = [low_half.astype(F32).astype(BF16), (lane >= DH).astype(F32).astype(BF16)]
    row2 = lax.broadcasted_iota(jnp.int32, (2 * UNIT, UNIT), 0) % UNIT
    col2 = lax.broadcasted_iota(jnp.int32, (2 * UNIT, UNIT), 1)
    seen = (row2 // BLK == col2 // BLK) & (col2 <= row2)

    def attend(j):
        def project(r, carry):
            rows = rows_of(r * 256, 256)
            acc = dot(a_ref[rows, :], bufs[0][j])
            qkv[j, rows, :] = acc[:, : 3 * wide].astype(BF16)
            u_ref[j, rows, :] = acc[:, 3 * wide :]
            return carry

        lax.fori_loop(0, TT // 256, project, 0)

        def unit(t, carry):
            rows = rows_of(t * UNIT, UNIT)
            for pair in range(wide // UNIT):
                q, k, v = (qkv[j, rows, pl.ds(f * wide + pair * UNIT, UNIT)] for f in range(3))
                cols = pl.ds(pair * UNIT, UNIT)
                scores = dot_nt(jnp.concatenate([q * keep[0], q * keep[1]], axis=0), k) * DH ** (-0.5)
                scores = jnp.where(seen, scores, -1e30)
                shifted = jnp.exp(scores - jnp.max(scores, axis=-1, keepdims=True))
                soft = (shifted / jnp.sum(shifted, axis=-1, keepdims=True)).astype(BF16)
                p_ref[j, pair, t] = soft
                attended = dot(
                    jnp.concatenate([soft[:UNIT], soft[UNIT:]], axis=1),
                    jnp.concatenate([v * keep[0], v * keep[1]], axis=0),
                )
                o_ref[j, rows, cols] = attended
                square = attended * attended
                mean0 = jnp.sum(jnp.where(low_half, square, 0.0), axis=-1, keepdims=True) / DH
                mean1 = jnp.sum(jnp.where(low_half, 0.0, square), axis=-1, keepdims=True) / DH
                normed = attended * lax.rsqrt(jnp.where(low_half, mean0, mean1) + EPSILON)
                u = u_ref[j, rows, cols]
                g = gain[j, 0:1, cols]
                z_ref[j, rows, cols] = (normed * g * (u * jax.nn.sigmoid(u))).astype(BF16)
            return carry

        lax.fori_loop(0, TT // UNIT, unit, 0)

    pump(until=3)
    attend(0)
    pump(number=3)
    attend(1)
    pump(until=4)
    for src, dst in ((qkv, qkv_out), (u_ref, u_out), (o_ref, o_out), (p_ref, p_out), (z_ref, z_out), (gain, gain_out)):
        save(src, dst)
    save(bufs[0], w_out[0])
    save(bufs[1], w_out[1])

    def out_rows(row):
        rows = rows_of(row, 256)
        return dot(z_ref[0, rows, :], bufs[1][0]) + dot(z_ref[1, rows, :], bufs[1][1])

    swaps = []
    for i in range(T // 256):
        hs[pl.ds(i * 256, 256), :] = out_rows(T + i * 256)
        part_rows = pl.ds(i * 256, 256)
        swaps.append(remote(hs.at[part_rows, :], hr.at[part_rows, :], es.at[2 + i], er.at[2 + i], me.sib))
        swaps[-1].start()
    for i in range(T // 256):
        h_ref[pl.ds(i * 256, 256), :] = x_ref[pl.ds(i * 256, 256), :].astype(F32) + out_rows(i * 256)
    pump(number=3)
    for i, swap in enumerate(list(swaps)):
        swap.wait_recv()

        def add_rows(t, carry):
            rows = rows_of(i * 256 + t * UNIT, UNIT)
            values = h_ref[rows, :] + hr[rows, :]
            h_ref[rows, :] = values
            b_ref[rows, :] = (values * rms_factor(values)).astype(BF16)
            return carry

        lax.fori_loop(0, 256 // UNIT, add_rows, 0)
        b_rows = pl.ds(i * 256, 256)
        swaps.append(remote(b_ref.at[b_rows, :], b_ref.at[pl.ds(T + i * 256, 256), :], es.at[4 + i], er.at[4 + i], me.sib))
        swaps[-1].start()
    save(h_ref, h_out)
    pump(number=3)
    for swap in swaps[len(swaps) // 2 :]:
        swap.wait_recv()
    save(b_ref, b_out)

    first_parts = [k for k in range(count) if plan[k][1] == 2]
    second_parts = [k for k in range(count) if plan[k][1] == 3]
    third_parts = [k for k in range(count) if plan[k][1] == 4]

    def rows_loop(body):
        lax.fori_loop(0, TT // 256, lambda r, carry: (body(rows_of(r * 256, 256)), carry)[1], 0)

    pump(until=first_parts[-1])
    save(bufs[2], w_out[2])
    for j in (0, 1):
        def first(rows):
            d2[j, rows, :] = dot(b_ref[rows, :], bufs[2][j]).astype(BF16)

        rows_loop(first)
        pump(number=2)
    pump(until=second_parts[-1])
    save(bufs[3], w_out[3])
    for j in (0, 1):
        def second(rows):
            g2 = dot(b_ref[rows, :], bufs[3][j])
            d1[j, rows, :] = g2.astype(BF16)
            m_ref[j, rows, :] = (d2[j, rows, :].astype(F32) * g2).astype(BF16)

        rows_loop(second)
        pump(number=2)
    save(m_ref, m_out)
    mine[1].wait()
    both[1].wait_recv()
    save(cot, cot_out)
    pump(until=third_parts[-1])
    save(bufs[4], w_out[4])
    for j in (0, 1):
        def third(rows):
            dm = dot_nt(cot[rows, :], bufs[4][j])
            g2, g1 = d1[j, rows, :].astype(F32), d2[j, rows, :].astype(F32)
            d1[j, rows, :] = (dm * g2).astype(BF16)
            d2[j, rows, :] = (dm * g1).astype(BF16)

        rows_loop(third)
        save(d1.at[j], d1_out.at[j])
        save(d2.at[j], d2_out.at[j])

    @pl.when(innet)
    def _():
        for d, inside in ((0, z < 3), (1, z > 0)):
            @pl.when(inside)
            def _():
                gain_copy(own, d, gain_in).wait_send()
                for k in range(count):
                    z_first(k, d).wait_send()

    def ends(j):
        @pl.when(upward(j) | downward(j))
        def _():
            for k in range(count):
                z_next(k, j, 0).wait_send()

        @pl.when(upward(j))
        def _():
            gain_copy(j, 0, gain.at[j]).wait_send()

        @pl.when(downward(j))
        def _():
            gain_copy(j, 1, gain.at[j]).wait_send()

        for k in range(count):
            for copy in (to_x, to_y, x_then_y, y_then_x):
                copy(k, j).wait_send()

    others(ends)
    for copy in both + swaps:
        copy.wait_send()
    for copy in saves:
        copy.wait()


def any_spec(count):
    return [pl.BlockSpec(memory_space=pl.ANY)] * count


def run_forward(x, cot, gain, weights):
    T, D = x.shape
    TT = 2 * T
    shapes = [w.shape for w in weights]
    plan = gather_plan(shapes)
    wide, hidden = shapes[0][1], shapes[5][1]
    units, pairs = TT // UNIT, wide // UNIT
    buffers = [(2, D, 4 * wide), (2, wide, D), (2, D, hidden), (2, D, hidden), (2, hidden, D)]
    kept = [
        ((TT, D), BF16),
        ((2, TT, 3 * wide), BF16),
        ((2, TT, wide), F32),
        ((2, TT, wide), F32),
        ((2, pairs, units, 2 * UNIT, UNIT), BF16),
        ((2, TT, wide), BF16),
        ((T, D), F32),
        ((TT, D), BF16),
        ((2, TT, hidden), BF16),
        ((2, TT, hidden), BF16),
        ((2, TT, hidden), BF16),
        ((TT, D), BF16),
        ((2, 8, wide), F32),
    ]
    vmem = [pltpu.VMEM(s, BF16) for s in buffers] + [
        pltpu.VMEM((TT, D), BF16),
        pltpu.VMEM((TT, D), BF16),
        pltpu.VMEM((TT, D), BF16),
        pltpu.VMEM((2, TT, 3 * wide), BF16),
        pltpu.VMEM((2, TT, wide), F32),
        pltpu.VMEM((2, TT, wide), F32),
        pltpu.VMEM((2, pairs, units, 2 * UNIT, UNIT), BF16),
        pltpu.VMEM((2, TT, wide), BF16),
        pltpu.VMEM((T, D), F32),
        pltpu.VMEM((T, D), F32),
        pltpu.VMEM((T, D), F32),
        pltpu.VMEM((TT, D), BF16),
        pltpu.VMEM((2, TT, hidden), BF16),
        pltpu.VMEM((2, TT, hidden), BF16),
        pltpu.VMEM((2, TT, hidden), BF16),
        pltpu.VMEM((2, 8, wide), F32),
    ]
    n = len(plan)
    dma = pltpu.SemaphoreType.DMA
    sems = [dma((n, 2))] * 7 + [dma((2, n, 2))] * 2 + [dma((11,)), dma((2, 2)), dma((2,)), dma((6,)), dma((6,)), dma((24,))]
    return pl.pallas_call(
        functools.partial(forward_kernel, plan, shapes),
        out_shape=[jax.ShapeDtypeStruct(s, BF16) for s in buffers] + [jax.ShapeDtypeStruct(s, t) for s, t in kept],
        in_specs=any_spec(3 + len(weights)),
        out_specs=any_spec(len(buffers) + len(kept)),
        scratch_shapes=vmem + sems,
        compiler_params=pltpu.CompilerParams(collective_id=0, has_side_effects=True, vmem_limit_bytes=VMEM_LIMIT),
        cost_estimate=pl.CostEstimate(flops=16 * 10**9, bytes_accessed=80 * 10**6, transcendentals=10**6),
        name="forward",
    )(x, cot, gain, *weights)


def backward_kernel(shapes, spare, *refs):
    (x_in, w0_in, wo_in, w1_in, w2_in, w3_in, a_in, qkv_in, u_in, o_in, p_in, z_in, h_in, b_in, m_in, d1_in, d2_in) = refs[:17]
    cot_in, gain_in = refs[17:19]
    out_out, dx_out = refs[19:21]
    final = refs[21:26]
    gain_out = refs[26]
    scratch = refs[27:]
    if spare:
        rq, scratch = scratch[:5], scratch[5:]
    gb, ra1, rb1, ra2, rb2, rz = (scratch[5 * i : 5 * i + 5] for i in range(6))
    (hs, hr, es_da, er_da, er_out, dh, dhl, gacc, gx, gy, gz, gq, stage) = scratch[30:43]
    (s1, r1, s2, r2, sz, rzs, sx, rx, sy, ry, sf, rf, ss, rs, sq, rqs, ld, es, er, gss, grs) = scratch[43:]
    me = Place()
    z, c, own, innet, p = me.z, me.c, me.own, me.innet, me.p
    bx, by = me.bx, me.by
    T, D = x_in.shape
    TT = 2 * T
    wide = wo_in.shape[1]
    hidden = w1_in.shape[2]
    arrays = range(5)

    def other_quad(e):
        bit = 8 << e
        return (me.dp + bit - 2 * bit * ((me.dp // bit) % 2), z)

    def other_z(t):
        return (me.dp, lax.rem(z + t, 4))

    bar = pltpu.get_barrier_semaphore()
    greeted = [me.sib, me.xn, me.yn] + [other_z(t) for t in (1, 2, 3)] + [other_quad(e) for e in range(spare)]
    for d in greeted:
        pl.semaphore_signal(bar, inc=1, device_id=d, device_id_type=MESH)
    pl.semaphore_wait(bar, len(greeted))

    quarters = [s[0] // 4 for s in shapes]
    halves = [half_of(q) for q in quarters]

    def add_rows(dst, sources, rows):
        def body(t, carry):
            r = rows_of(t * 16, 16)
            total = dst[r, :].astype(F32)
            for src in sources:
                total = total + src[r, :].astype(F32)
            dst[r, :] = total.astype(BF16)
            return carry

        lax.fori_loop(0, rows // 16, body, 0)

    def first_half(i, j, who):
        return gb[i].at[j, rows_of(who * quarters[i], halves[i]), :]

    def second_half(i, j, who):
        return gb[i].at[j, rows_of(who * quarters[i] + halves[i], quarters[i] - halves[i]), :]

    def whole(i, j, who):
        return gb[i].at[j, rows_of(who * quarters[i], quarters[i]), :]

    def round1(i, j):
        copies = []
        for b in (0, 1):
            copies.append(
                remote(first_half(i, j, b * 2 + 1 - bx), ra1[i].at[j, b], s1.at[i, j, b], r1.at[i, j, b], me.xn)
            )
            copies.append(
                remote(second_half(i, j, (1 - by) * 2 + b), rb1[i].at[j, b], s1.at[i, j, 2 + b], r1.at[i, j, 2 + b], me.yn)
            )
        return copies

    def round2(i, j):
        return [
            remote(first_half(i, j, (1 - by) * 2 + bx), ra2[i].at[j], s2.at[i, j, 0], r2.at[i, j, 0], me.yn),
            remote(second_half(i, j, by * 2 + 1 - bx), rb2[i].at[j], s2.at[i, j, 1], r2.at[i, j, 1], me.xn),
        ]

    def round_z(i, j):
        slot = lax.rem(z - (2 * c + j) + 3 + 4, 4)
        return remote(whole(i, j, p), rz[i].at[slot], sz.at[i, j], rzs.at[i, slot], (me.dp, 2 * c + j))

    def landed_z(i, slot):
        return remote(rz[i].at[slot], rz[i].at[slot], sz.at[i, 0], rzs.at[i, slot], me.sib)

    def spread(i, j):
        src = whole(i, j, p)
        dst = final[i].at[rows_of(p * quarters[i], quarters[i]), :]
        return [
            remote(src, dst, sx.at[i], rx.at[i], me.xn),
            remote(src, dst, sy.at[i], ry.at[i], me.yn),
            remote(src, dst, ss.at[i, 0], rs.at[i, 0], me.sib),
        ], pltpu.make_async_copy(src, dst, ld.at[32 + i])

    def quarter_rows(i, who, second=None):
        q, h = quarters[i], halves[i]
        if second is None:
            return final[i].at[rows_of(who * q, q), :]
        if second:
            return final[i].at[rows_of(who * q + h, q - h), :]
        return final[i].at[rows_of(who * q, h), :]

    def hand_on(i, slot, ref):
        return remote(ref, ref, ss.at[i, slot], rs.at[i, slot], me.sib)

    def pass_x(i):
        r = quarter_rows(i, me.px, False)
        return remote(r, r, sf.at[i, 0], rf.at[i, 0], me.yn), hand_on(i, 1, quarter_rows(i, me.px))

    def pass_y(i):
        r = quarter_rows(i, me.py, True)
        return remote(r, r, sf.at[i, 1], rf.at[i, 1], me.xn), hand_on(i, 2, quarter_rows(i, me.py))

    def pass_last(i):
        return hand_on(i, 3, quarter_rows(i, me.pd, False)), hand_on(i, 4, quarter_rows(i, me.pd, True))

    def step_1(i, j):
        for copy in round1(i, j):
            copy.start()

    def step_2(i, j):
        for copy in round1(i, j):
            copy.wait_recv()
        add_rows(first_half(i, j, (1 - by) * 2 + bx), [ra1[i].at[j, 1 - by]], halves[i])
        add_rows(second_half(i, j, by * 2 + 1 - bx), [rb1[i].at[j, 1 - bx]], quarters[i] - halves[i])
        for copy in round2(i, j):
            copy.start()

    def step_3(i, j):
        for copy in round2(i, j):
            copy.wait_recv()
        add_rows(first_half(i, j, p), [ra1[i].at[j, by], ra2[i].at[j]], halves[i])
        add_rows(second_half(i, j, p), [rb1[i].at[j, bx], rb2[i].at[j]], quarters[i] - halves[i])

        @pl.when(z != 2 * c + j)
        def _():
            round_z(i, j).start()

    def step_4(i, j):
        @pl.when(z == 2 * c + j)
        def _():
            for slot in range(3):
                landed_z(i, slot).wait_recv()
            add_rows(whole(i, j, p), [rz[i].at[slot] for slot in range(3)], quarters[i])
            for e in range(spare):
                copy = remote(whole(i, j, p), rq[i].at[e], sq.at[i, e], rqs.at[i, e], other_quad(e))
                copy.start()
                copy.wait()
                h = halves[i]
                for k, (part, src) in enumerate(
                    ((ra2[i].at[j], rq[i].at[e, pl.ds(0, h), :]), (rb2[i].at[j], rq[i].at[e, pl.ds(h, quarters[i] - h), :]))
                ):
                    local = pltpu.make_async_copy(src, part, sq.at[i, k])
                    local.start()
                    local.wait()
                add_rows(first_half(i, j, p), [ra2[i].at[j]], h)
                add_rows(second_half(i, j, p), [rb2[i].at[j]], quarters[i] - h)
            copies, local = spread(i, j)
            for copy in copies:
                copy.start()
            local.start()

    def step_5(i, j):
        @pl.when(z == 2 * c + j)
        def _():
            copies, _ = spread(i, j)
            copies[0].wait_recv()
            for copy in pass_x(i):
                copy.start()
            copies[1].wait_recv()
            for copy in pass_y(i):
                copy.start()

    def step_6(i, j):
        @pl.when(z == 2 * c + j)
        def _():
            pass_x(i)[0].wait_recv()
            pass_y(i)[0].wait_recv()
            for copy in pass_last(i):
                copy.start()

    items = [(4, 0), (4, 1), (2, 0), (2, 1), (3, 0), (3, 1), (1, 0), (1, 1), (0, 0), (0, 1)]
    steps = []
    stages = ((step_2, 2), (step_3, 4), (step_4, 6), (step_5, 7), (step_6, 8))
    for t in range(len(items) + 9):
        for step, lag in stages:
            if 0 <= t - lag < len(items):
                steps.append((step, items[t - lag]))
    sent = [0]
    done = [0]

    def send(i, j):
        step_1(i, j)
        sent[0] += 1

    def pump(number):
        while done[0] < len(steps) and number > 0:
            step, item = steps[done[0]]
            if items.index(item) >= sent[0]:
                return
            step(*item)
            done[0] += 1
            number -= 1

    loads = [0]

    def load(src, dst):
        copy = pltpu.make_async_copy(src, dst, ld.at[loads[0]])
        copy.start()
        loads[0] += 1
        return copy

    h_load = load(h_in, stage.at[0])

    def loop(count, body):
        lax.fori_loop(0, count, lambda t, carry: (body(t), carry)[1], 0)

    def feed_forward(b_ref, d1, d2):
        b_load, d1_load, d2_load = load(b_in, b_ref), load(d1_in, d1), load(d2_in, d2)

        def third(m_ref, cot):
            for copy in (load(m_in, m_ref), load(cot_in, cot)):
                copy.wait()
            for j in (0, 1):
                for start in range(0, hidden, 256):
                    size = min(256, hidden - start)
                    gb[4][j, pl.ds(start, size), :] = dot_tn(m_ref[j, :, pl.ds(start, size)], cot[...]).astype(BF16)
                send(4, j)

        pl.run_scoped(third, pltpu.VMEM((2, TT, hidden), BF16), pltpu.VMEM((TT, D), BF16))

        def first_two(w1, w2):
            w_loads = [load(w1_in, w1), load(w2_in, w2)]
            for copy in (b_load, d1_load, d2_load):
                copy.wait()
            for i, d in ((2, d1), (3, d2)):
                for j in (0, 1):
                    def block(t):
                        rows = pl.ds(pl.multiple_of(t * 256, 256), 256)
                        gb[i][j, rows, :] = dot_tn(b_ref[:, rows], d[j]).astype(BF16)

                    loop(D // 256, block)
                    send(i, j)
                    pump(1 if i == 2 else 2)
            for copy in w_loads:
                copy.wait()

            def db_rows(row):
                rows = rows_of(row, 256)
                total = dot_nt(d1[0, rows, :], w1[0]) + dot_nt(d2[0, rows, :], w2[0])
                return total + dot_nt(d1[1, rows, :], w1[1]) + dot_nt(d2[1, rows, :], w2[1])

            for t in range(T // 256):
                part = pl.ds(t * 256, 256)
                hs[part, :] = db_rows(T + t * 256)
                swap(t).start()
                pump(1)
            for t in range(T // 256):
                dh[pl.ds(t * 256, 256), :] = db_rows(t * 256)
                pump(1)

        pl.run_scoped(first_two, pltpu.VMEM((2, D, hidden), BF16), pltpu.VMEM((2, D, hidden), BF16))

    def swap(t):
        part = pl.ds(t * 256, 256)
        return remote(hs.at[part, :], hr.at[part, :], es.at[t], er.at[t], me.sib)

    def swap_low(t):
        part = pl.ds(t * 256, 256)
        return remote(dhl.at[part, :], dhl.at[pl.ds(T + t * 256, 256), :], es.at[2 + t], er.at[2 + t], me.sib)

    def swap_da(t):
        part = pl.ds(t * 256, 256)
        return remote(es_da.at[part, :], er_da.at[part, :], es.at[4 + t], er.at[4 + t], me.sib)

    def swap_out(t):
        part = pl.ds(t * 256, 256)
        return remote(es_da.at[part, :], er_out.at[part, :], es.at[6 + t], er.at[6 + t], me.sib)

    pl.run_scoped(
        feed_forward, pltpu.VMEM((TT, D), BF16), pltpu.VMEM((2, TT, hidden), BF16), pltpu.VMEM((2, TT, hidden), BF16)
    )

    lane = lax.broadcasted_iota(jnp.int32, (UNIT, UNIT), 1)
    low_half = lane < DH
    keep = [low_half.astype(F32).astype(BF16), (lane >= DH).astype(F32).astype(BF16)]

    def stacked(values):
        return jnp.concatenate([values * keep[0], values * keep[1]], axis=0)

    def head_mean(values):
        mean0 = jnp.sum(jnp.where(low_half, values, 0.0), axis=-1, keepdims=True) / DH
        mean1 = jnp.sum(jnp.where(low_half, 0.0, values), axis=-1, keepdims=True) / DH
        return jnp.where(low_half, mean0, mean1)

    def attention(dproj, a_ref):
        a_load = load(a_in, a_ref)

        def inner(qkv, u_ref, o_ref, p_ref, wo, gain):
            copies = [
                load(src, dst)
                for src, dst in (
                    (cot_in.at[pl.ds(0, T), :], es_da), (wo_in, wo), (u_in, u_ref),
                    (o_in, o_ref), (p_in, p_ref), (qkv_in, qkv), (gain_in, gain),
                )
            ]
            h_load.wait()
            copies[0].wait()
            for t in range(T // 256):
                swap(t).wait_recv()

                def rows_body(r):
                    rows = rows_of(t * 256 + r * 64, 64)
                    db = dh[rows, :] + hr[rows, :]
                    h = stage[0, rows, :]
                    factor = rms_factor(h)
                    normed = h * factor
                    grad = es_da[rows, :].astype(F32) + factor * (
                        db - normed * jnp.mean(db * normed, axis=-1, keepdims=True)
                    )
                    dh[rows, :] = grad
                    dhl[rows, :] = grad.astype(BF16)

                loop(4, rows_body)
                swap_low(t).start()
                pump(1)
            for copy in copies[1:]:
                copy.wait()
            gacc[...] = jnp.zeros_like(gacc)

            def out_grads(z_ref):
                z_load = load(z_in, z_ref)
                for t in range(T // 256):
                    swap_low(t).wait_recv()
                z_load.wait()
                for j in (0, 1):
                    gb[1][j] = dot_tn(z_ref[j], dhl[...]).astype(BF16)
                    send(1, j)
                    pump(1)

            pl.run_scoped(out_grads, pltpu.VMEM((2, TT, wide), BF16))
            pl.run_scoped(functools.partial(heads, qkv, u_ref, o_ref, p_ref, wo, gain), pltpu.VMEM((TT, wide), F32))

        def heads(qkv, u_ref, o_ref, p_ref, wo, gain, dz_ref):
            for j in (0, 1):
                def dz_rows(t):
                    rows = rows_of(t * 256, 256)
                    dz_ref[rows, :] = dot_nt(dhl[rows, :], wo[j])

                loop(TT // 256, dz_rows)

                def unit(t):
                    rows = rows_of(t * UNIT, UNIT)
                    for pair in range(wide // UNIT):
                        cols = pl.ds(pair * UNIT, UNIT)
                        q, k, v = (qkv[j, rows, pl.ds(f * wide + pair * UNIT, UNIT)] for f in range(3))
                        o, u, dz = o_ref[j, rows, cols], u_ref[j, rows, cols], dz_ref[rows, cols]
                        gain_row = gain[j, 0:1, cols]
                        factor = lax.rsqrt(head_mean(o * o) + EPSILON)
                        normed = o * factor
                        s = jax.nn.sigmoid(u)
                        act = u * s
                        dzn = dz * normed
                        gacc[j, :, cols] += jnp.sum((dzn * act).reshape(UNIT // 8, 8, UNIT), axis=0)
                        du = (dzn * gain_row * s * (1.0 + u * (1.0 - s))).astype(BF16)
                        dn = dz * act * gain_row
                        do = stacked((factor * (dn - normed * head_mean(dn * normed))).astype(BF16))
                        soft_low = p_ref[j, pair, t]
                        soft = soft_low.astype(F32)
                        dv = dot_tn(soft_low, do)
                        dp = dot_nt(do, v)
                        ds = (soft * (dp - jnp.sum(dp * soft, axis=-1, keepdims=True))).astype(BF16)
                        dq = dot(jnp.concatenate([ds[:UNIT], ds[UNIT:]], axis=1), stacked(k)) * DH ** (-0.5)
                        dk = dot_tn(ds, stacked(q)) * DH ** (-0.5)
                        for f, value in enumerate((dq, dk, dv)):
                            dproj[j, rows, pl.ds(f * wide + pair * UNIT, UNIT)] = value.astype(BF16)
                        dproj[j, rows, pl.ds(3 * wide + pair * UNIT, UNIT)] = du

                loop(TT // UNIT, unit)
                if j == 0:
                    a_load.wait()
                pump(1)

                def block(t):
                    rows = pl.ds(pl.multiple_of(t * 256, 256), 256)
                    gb[0][j, rows, :] = dot_tn(a_ref[:, rows], dproj[j]).astype(BF16)

                loop(D // 256, block)
                send(0, j)
                pump(2)

        pl.run_scoped(
            inner,
            pltpu.VMEM((2, TT, 3 * wide), BF16),
            pltpu.VMEM((2, TT, wide), F32),
            pltpu.VMEM((2, TT, wide), F32),
            pltpu.VMEM((2, wide // UNIT, TT // UNIT, 2 * UNIT, UNIT), BF16),
            pltpu.VMEM((2, wide, D), BF16),
            pltpu.VMEM((2, 8, wide), F32),
        )

        def inputs_part(w0, x_ref):
            for copy in (load(w0_in, w0), load(x_in, x_ref)):
                copy.wait()

            def da_rows(row):
                rows = rows_of(row, 256)
                return dot_nt(dproj[0, rows, :], w0[0]) + dot_nt(dproj[1, rows, :], w0[1])

            for t in range(T // 256):
                es_da[pl.ds(t * 256, 256), :] = da_rows(T + t * 256).astype(BF16)
                swap_da(t).start()
                pump(1)
            for t in range(T // 256):
                hs[pl.ds(t * 256, 256), :] = da_rows(t * 256)
                pump(1)
            for t in range(T // 256):
                swap_da(t).wait_recv()

                def rows_body(r):
                    rows = rows_of(t * 256 + r * 64, 64)
                    da = hs[rows, :] + er_da[rows, :].astype(F32)
                    x = x_ref[rows, :].astype(F32)
                    factor = rms_factor(x)
                    normed = x * factor
                    dh[rows, :] = dh[rows, :] + factor * (
                        da - normed * jnp.mean(da * normed, axis=-1, keepdims=True)
                    )

                loop(4, rows_body)
                pump(1)

        for t in range(T // 256):
            swap(t).wait_send()
        pl.run_scoped(inputs_part, pltpu.VMEM((2, D, 4 * wide), BF16), pltpu.VMEM((T, D), BF16))

    pl.run_scoped(attention, pltpu.VMEM((2, TT, 4 * wide), BF16), pltpu.VMEM((TT, D), BF16))
    dx_save = load(dh, dx_out)

    def gain_sum(k, src, dst, device, total):
        copy = remote(src, dst, gss.at[k], grs.at[k], device)
        copy.start()
        copy.wait()
        total[...] += dst[...]

    gain_sum(0, gacc, gx, me.xn, gacc)
    pump(2)
    gain_sum(1, gacc, gy, me.yn, gacc)

    def gain_z(j):
        slot = lax.rem(z - (2 * c + j) + 3 + 4, 4)
        return remote(gacc.at[j], gz.at[slot], gss.at[2 + j], grs.at[4 + slot], (me.dp, 2 * c + j))

    for j in (0, 1):
        @pl.when(z != 2 * c + j)
        def _():
            gain_z(j).start()

    def output_part(m_ref, w3):
        for copy in (load(m_in, m_ref), load(w3_in, w3)):
            copy.wait()
        for t in range(T // 256):
            swap_da(t).wait_send()

        def out_rows(row):
            rows = rows_of(row, 256)
            return dot(m_ref[0, rows, :], w3[0]) + dot(m_ref[1, rows, :], w3[1])

        for t in range(T // 256):
            es_da[pl.ds(t * 256, 256), :] = out_rows(T + t * 256).astype(BF16)
            swap_out(t).start()
            pump(1)
        for t in range(T // 256):
            rows = pl.ds(t * 256, 256)
            stage[0, rows, :] = stage[0, rows, :] + out_rows(t * 256)
            pump(1)
        for t in range(T // 256):
            swap_out(t).wait_recv()
            rows = pl.ds(t * 256, 256)
            stage[0, rows, :] = stage[0, rows, :] + er_out[rows, :].astype(F32)

    pl.run_scoped(output_part, pltpu.VMEM((2, TT, hidden), BF16), pltpu.VMEM((2, hidden, D), BF16))
    out_save = load(stage.at[0], out_out)

    def gain_final():
        return remote(gacc.at[own], gain_out, gss.at[7], grs.at[7], me.sib)

    @pl.when(innet)
    def _():
        for slot in range(3):
            remote(gz.at[slot], gz.at[slot], gss.at[2], grs.at[4 + slot], me.sib).wait_recv()
            gacc[own] += gz[slot]
        for e in range(spare):
            copy = remote(gacc.at[own], gq.at[e], gss.at[8 + e], grs.at[8 + e], other_quad(e))
            copy.start()
            copy.wait()
            gacc[own] += gq[e]
        local = pltpu.make_async_copy(gacc.at[own], gain_out, ld.at[37])
        local.start()
        gain_final().start()
        local.wait()
        gain_final().wait_send()

    pump(len(steps))

    @pl.when(jnp.logical_not(innet))
    def _():
        gain_final().wait_recv()
        for i in arrays:
            spread(i, 0)[0][2].wait_recv()
            pass_x(i)[1].wait_recv()
            pass_y(i)[1].wait_recv()
            for copy in pass_last(i):
                copy.wait_recv()

    @pl.when(innet)
    def _():
        for i in arrays:
            copies, local = spread(i, own)
            for copy in copies:
                copy.wait_send()
            local.wait()
            for copies in (pass_x(i), pass_y(i), pass_last(i)):
                for copy in copies:
                    copy.wait_send()

    for i, j in items:
        for copy in round1(i, j) + round2(i, j):
            copy.wait_send()

        @pl.when(z != 2 * c + j)
        def _():
            round_z(i, j).wait_send()

    for j in (0, 1):
        @pl.when(z != 2 * c + j)
        def _():
            gain_z(j).wait_send()

    for t in range(T // 256):
        swap_low(t).wait_send()
        swap_out(t).wait_send()
    dx_save.wait()
    out_save.wait()


def run_backward(x, kept, spare):
    T, D = x.shape
    TT = 2 * T
    w0, wo, w1, w2, w3 = kept[:5]
    wide, hidden = wo.shape[1], w1.shape[2]
    shapes = [w.shape[1:] for w in (w0, wo, w1, w2, w3)]
    q = [s[0] // 4 for s in shapes]
    h = [half_of(n) for n in q]
    cols = [s[1] for s in shapes]
    n = range(5)
    extra = max(spare, 1)
    vmem = (
        [pltpu.VMEM((2,) + s, BF16) for s in shapes]
        + [pltpu.VMEM((2, 2, h[i], cols[i]), BF16) for i in n]
        + [pltpu.VMEM((2, 2, q[i] - h[i], cols[i]), BF16) for i in n]
        + [pltpu.VMEM((2, h[i], cols[i]), BF16) for i in n]
        + [pltpu.VMEM((2, q[i] - h[i], cols[i]), BF16) for i in n]
        + [pltpu.VMEM((3, q[i], cols[i]), BF16) for i in n]
        + [
            pltpu.VMEM((T, D), F32),
            pltpu.VMEM((T, D), F32),
            pltpu.VMEM((T, D), BF16),
            pltpu.VMEM((T, D), BF16),
            pltpu.VMEM((T, D), BF16),
            pltpu.VMEM((T, D), F32),
            pltpu.VMEM((TT, D), BF16),
            pltpu.VMEM((2, 8, wide), F32),
            pltpu.VMEM((2, 8, wide), F32),
            pltpu.VMEM((2, 8, wide), F32),
            pltpu.VMEM((3, 8, wide), F32),
            pltpu.VMEM((extra, 8, wide), F32),
            pltpu.VMEM((1, T, D), F32),
        ]
    )
    dma = pltpu.SemaphoreType.DMA
    sems = [
        dma((5, 2, 4)), dma((5, 2, 4)), dma((5, 2, 2)), dma((5, 2, 2)), dma((5, 2)), dma((5, 3)),
        dma((5,)), dma((5,)), dma((5,)), dma((5,)), dma((5, 2)), dma((5, 2)), dma((5, 5)), dma((5, 5)),
        dma((5, 2 + extra)), dma((5, extra)), dma((38,)), dma((8,)), dma((8,)), dma((8 + extra,)), dma((8 + extra,)),
    ]
    outs = [((T, D), F32), ((T, D), F32)] + [(s, BF16) for s in shapes] + [((8, wide), F32)]
    if spare:
        outs += [((spare, q[i], cols[i]), BF16) for i in n]
    return pl.pallas_call(
        functools.partial(backward_kernel, shapes, spare),
        out_shape=[jax.ShapeDtypeStruct(s, t) for s, t in outs],
        in_specs=any_spec(1 + len(kept)),
        out_specs=any_spec(len(outs)),
        scratch_shapes=vmem + sems,
        compiler_params=pltpu.CompilerParams(collective_id=1, has_side_effects=True, vmem_limit_bytes=VMEM_LIMIT),
        cost_estimate=pl.CostEstimate(flops=30 * 10**9, bytes_accessed=80 * 10**6, transcendentals=10**6),
        name="backward",
    )(x, *kept)


def shards(
    inputs, w_query, w_key, w_value, w_gate, head_gain, w_out, w_first, w_second, w_third, cotangent
):
    wide = w_query.shape[1]
    weights = [w_query, w_key, w_value, w_gate, w_out, w_first, w_second, w_third]
    gain = jnp.broadcast_to(head_gain[None], (8, wide))
    kept = run_forward(inputs, cotangent, gain, weights)
    spare = (lax.axis_size("dp") // 8).bit_length() - 1
    output, grad_inputs, g_in, g_out, g_first, g_second, g_third, g_gain = run_backward(inputs, kept, spare)[:8]
    return (
        output,
        grad_inputs,
        *(g_in[:, i * wide : (i + 1) * wide].astype(F32) for i in range(4)),
        jnp.sum(g_gain, axis=0),
        *(g.astype(F32) for g in (g_out, g_first, g_second, g_third)),
    )


def solution(mesh):
    rows, columns = P(("dp", "mp"), None), P(None, "mp")
    heads = P("mp", None)
    return jax.shard_map(
        shards,
        mesh=mesh,
        in_specs=(rows, columns, columns, columns, columns, P("mp"), heads, columns, columns, heads, rows),
        out_specs=(rows, rows, columns, columns, columns, columns, P("mp"), heads, columns, columns, heads),
        check_vma=False,
    )
```

time: 1190 us -> 344 us (0.29)
  waiting for transfers between devices: 806 us -> 0 us
  Pallas kernels: 0 us -> 316 us
  matrix products: 127 us -> 0 us
  local copies, waits for them, and re-layouts: 122 us -> 14.1 us
  blocking collectives: 60 us -> 0 us
  other arithmetic: 47.7 us -> 7.59 us
  between operations: 15.2 us -> 0.69 us
    reduce_scatter x3 -> x0, waiting for transfers between devices: 371 us -> none  [reduce_gradient(): lax.psum_scatter(stacked.reshape(shards_ * rows, columns), ALL, scatter_d...]
    all_gather x9 -> x0, waiting for transfers between devices: 339 us -> none  [the longest x5 253 us: gather_weight(): full = lax.all_gather(part, ALL, axis=0, tiled=True)]
    pallas_call x0 -> x2, Pallas kernels: none -> 316 us  [the longest x1 200 us: run_backward(): pl.pallas_call(functools.partial(backward_kernel, shapes, spare), out_sha...]
    dot_general x47 -> x0, matrix products: 122 us -> none  [the longest x14 37.6 us: matmul_nt(): lax.dot_general(left, right, (((1,), (1,)), ((), ())), preferred_element_...]
    unnamed x16 -> x0, waiting for transfers between devices: 95.9 us -> none
    convert_element_type x11 -> x0, local copies, waits for them, and re-layouts: 40.6 us -> none  [the longest x2 8.47 us: shards(): key_rows = field(1).astype(low)]
    psum x1 -> x0, blocking collectives: 37.3 us -> none  [shards(): grad_head_gain = lax.psum(grad_head_gain, ALL)]
    all_gather x2 -> x0, blocking collectives: 22.7 us -> none  [the longest x1 12.7 us: shards(): gain = lax.all_gather(head_gain, 'mp', axis=0, tiled=True)]
  transfers between devices with their start and end apart: 14 -> 0, of which waited for: 12 -> 0; matrix products, arithmetic and copies ran while one was open for 22% -> 0% of each run, Pallas kernels for 0% -> 0%
where the time goes in v3:
time: 344 us; the launch traced here: 338 us
  Pallas kernels  316 us (92%)
  local copies, waits for them, and re-layouts  14.1 us (4%)
  other arithmetic  7.59 us (2%)
    pallas_call x1, Pallas kernels, run_backward(): pl.pallas_call(functools.partial(backward_kernel, shapes, spare), out_sha...  200 us
    pallas_call x1, Pallas kernels, run_forward(): pl.pallas_call(functools.partial(forward_kernel, plan, shapes), out_shape...  116 us
    unnamed x20, local copies, waits for them, and re-layouts  12.7 us

profile of v3, /device:TPU:0, one launch (start us, length us, event | category | flops | bytes accessed | tf_op | source)
XLA Modules:
  0.0 338.3 jit_solution(5439304790713373945)
XLA Ops:
  0.6 0.0 copy-start.5
  0.7 1.4 broadcast_in_dim.2.refs_2_
  2.0 2.6 copy.22.refs_8_
  4.6 0.0 copy-done.5
  4.6 1.6 copy.23.refs_9_
  6.2 115.5 %forward.1 = (bf16[2,1024,1024]{2,1,0:T(8,128)(2,1)}, bf16[2,256,1024]{2,1,0:T(8,128)(2,1)}, bf16[2,1024,704]{2,1,0:T(8,128)(2,1)}, bf16[2,1024,704]{2,1,0:T(8,1...) custom-call(bf16[512,1024]{1,0:T(8,128)(2,1)} %refs_0_.3, ...), custom_call_target="tpu_custom_call" | custom-call | flops 16000000000 | bytes 80000000 | tf_op jit(solution)/shard_map/forward/pallas_call | solution.py:510
  121.7 200.4 %backward.1 = (f32[512,1024]{1,0:T(8,128)}, f32[512,1024]{1,0:T(8,128)}, bf16[1024,1024]{1,0:T(8,128)(2,1)}, bf16[256,1024]{1,0:T(8,128)(2,1)}, bf16[1024,704]{1...) custom-call(bf16[512,1024]{1,0:T(8,128)(2,1)} %refs_0_.3, ...), custom_call_target="tpu_custom_call" | custom-call | flops 30000001024 | bytes 80000000 | tf_op jit(solution)/shard_map/backward/pallas_call | solution.py:1107
  322.1 0.0 copy-start.4
  322.1 1.4 reduce_sum.9
  323.5 2.1 convert_element_type.28
  325.6 0.0 copy-done.4
  325.6 0.0 copy-start.3
  325.6 2.0 copy.24
  327.6 0.0 copy-done.3
  327.6 0.0 copy-start.6
  327.6 2.0 copy.25
  329.5 0.0 copy-done.6
  329.5 0.0 copy-start
  329.5 1.9 convert_element_type.31
  331.5 0.3 copy-done
  331.7 0.0 copy-start.2
  331.7 2.1 slice_convert_fusion
  333.9 0.7 copy-done.2
  334.6 0.0 copy-start.1
  334.6 1.3 copy.28
  335.9 1.0 copy-done.1
  336.9 1.3 copy.29
Async XLA Ops:
  0.6 4.0 %copy-start.5 = (bf16[1024,704]{0,1:T(8,128)(2,1)S(1)}, bf16[1024,704]{0,1:T(8,128)(2,1)}, u32[]{:S(2)}) copy-start(bf16[1024,704]{0,1:T(8,128)(2,1)} %param.19) | copy-start | bytes 4325380
  322.1 3.5 %copy-start.4 = (bf16[1024,704]{1,0:T(8,128)(2,1)S(1)}, bf16[1024,704]{1,0:T(8,128)(2,1)}, u32[]{:S(2)}) copy-start(bf16[1024,704]{1,0:T(8,128)(2,1)} %get-tuple-element.60) | copy-start | bytes 4325380
  325.6 2.0 copy-start.3
  327.6 2.0 copy-start.6
  329.5 2.2 copy-start
  331.7 2.9 copy-start.2
  334.6 2.3 copy-start.1
